TPU v7x, 32 devices: a whole 2x2x4 slice. The times are simulated.
32 devices in a mesh: lon: 8 (over z, x), lat: 4 (over y, core).
Axes of the slice: x: 2, y: 2, z: 4, core: 2. Of those that a mesh axis runs over, the one named last changes fastest.
Arguments:
- tokens: bfloat16 [4, 24, 192, 192], P(None, 'lat', 'lon'), may hold values from -6 to 6
- cotangent: bfloat16 [4, 24, 192, 192], P(None, 'lat', 'lon'), may hold values from -6 to 6
- land_sea: int32 [24, 192], P('lat', 'lon'), may hold values 0 or 1
- land_vector: float32 [192], replicated, may hold values from -4 to 4
- triple_weight: bfloat16 [192, 576], replicated, may hold values from -0.4375 to 0.4375
- project_weight: bfloat16 [192, 192], replicated, may hold values from -0.4375 to 0.4375
- up_weight: bfloat16 [192, 768], replicated, may hold values from -0.4375 to 0.4375
- down_weight: bfloat16 [768, 192], replicated, may hold values from -0.21875 to 0.21875
- earth_bias: float32 [4, 2, 6, 144, 23], P('lat'), may hold values from -5 to 5
Outputs:
- grad_tokens: bfloat16 [4, 24, 192, 192], P(None, 'lat', 'lon')
- grad_triple: float32 [192, 576], replicated
- grad_project: float32 [192, 192], replicated
- grad_up: float32 [192, 768], replicated
- grad_down: float32 [768, 192], replicated
- grad_land: float32 [192], replicated
All inputs are finite; a program needn't handle non-finite values. No bound on the sum of `land_sea` on one device may be relied on, other than what follows from the above.
Results may differ from a plain program's by a relative error of at most 0.013.
Values may be sent and summed in bfloat16 or wider, within the bound.
No kernel may reach another device: no remote copies, remote signals or barrier semaphores. Data moves between devices by JAX's collectives and lax.ppermute only.
A program may use at most 128 MiB of HBM per device.

v0:
```python
import functools
import math

import jax
import jax.numpy as jnp
import numpy as np
from jax import lax
from jax.experimental import pallas as pl
from jax.experimental.pallas import tpu as pltpu
from jax.sharding import PartitionSpec as P

Z = 4
WZ = 2
WH = 6
WW = 12
C = 192
HEADS = 6
HEAD = 32
FF = 768
HZ, HH, HW = WZ // 2, WH // 2, WW // 2
TOK = WZ * WH * WW
PLACES = WZ * WH
RELW = 2 * WW - 1
SPOTS = PLACES // 2
STRIP = -(-RELW * SPOTS // 128) * 128
RUN, SHORT = WW * SPOTS, (WW - HW) * SPOTS

mask_fill = -10000.0
norm_eps = 1e-05
log2e = 1.4426950408889634
root_half = 0.7071067811865476
inv_root_tau = 0.3989422804014327
score_scale = HEAD**-0.5

f32 = jnp.float32
bf16 = jnp.bfloat16
MIB = 1 << 20

QUADS = 4
FAR_FIRST = range(QUADS - 1, 0, -1)
PART = C // (2 * QUADS)
CHUNK = 3 * PART
BLOCKS = FF // 128
EXTRA = 8
FULL = BLOCKS * CHUNK + EXTRA


def mm(a, b):
    return lax.dot_general(a, b, (((1,), (0,)), ((), ())), preferred_element_type=f32)


def mm_nt(a, b):
    return lax.dot_general(a, b, (((1,), (1,)), ((), ())), preferred_element_type=f32)


def mm_tn(a, b):
    return lax.dot_general(a, b, (((0,), (0,)), ((), ())), preferred_element_type=f32)


def unit_norm(values):
    average = jnp.mean(values, -1, keepdims=True)
    centred = values - average
    variance = jnp.mean(centred * centred, -1, keepdims=True)
    spread = lax.rsqrt(variance + norm_eps)
    return centred * spread, spread


def norm_back(upstream, unit, spread):
    first = jnp.mean(upstream, -1, keepdims=True)
    second = jnp.mean(upstream * unit, -1, keepdims=True)
    return spread * (upstream - first - unit * second)


def piece_rows(rows, cols):
    home = np.arange(Z * rows * cols).reshape(Z, rows, cols)

    def run(level, row, col, width):
        levels = [(level * WZ + z - HZ) % Z for z in range(WZ)]
        return home[levels, row : row + HH, col : col + width].transpose(2, 0, 1).reshape(-1)

    levels = range(Z // WZ)
    parts = []
    for row in (0, rows - HH):
        whole = [run(a, row, w * WW - HW, WW) for w in range(1, cols // WW) for a in levels]
        parts.append(np.concatenate(whole + [run(a, row, 0, WW - HW) for a in levels]))
    for row in (0, rows - HH):
        parts.append(np.concatenate([run(a, row, cols - HW, HW) for a in levels]))
    return parts


def window_runs(lon_windows):
    levels = Z // WZ
    whole = (lon_windows - 1) * levels
    runs = [[(1, n * RUN, RUN), (0, n * RUN, RUN)] for n in range(whole)]
    for a in range(levels):
        inner = whole * RUN + a * SHORT
        west = (a * (RUN - SHORT), RUN - SHORT)
        runs.append([(3, *west), (1, inner, SHORT), (2, *west), (0, inner, SHORT)])
    return runs


def spots(places):
    return jnp.asarray(np.argsort(places).astype(np.int32)[None])


def one_hot(spot_ref):
    count = spot_ref.shape[1]
    rows = lax.broadcasted_iota(jnp.int32, (count, count), 0)
    return (rows == spot_ref[...]).astype(f32).astype(bf16)


def vmem(count):
    return [pl.BlockSpec(memory_space=pltpu.VMEM)] * count


def shape(dims, dtype):
    return jax.ShapeDtypeStruct(dims, dtype)


def cost(flops, moved):
    return pl.CostEstimate(flops=flops, bytes_accessed=moved, transcendentals=0)


def land_column(land_ref, rows, cols):
    eye = (
        lax.broadcasted_iota(jnp.int32, (cols, cols), 0)
        == lax.broadcasted_iota(jnp.int32, (cols, cols), 1)
    ).astype(f32)
    land = land_ref[...].astype(f32)
    parts = [jnp.sum(eye * land[i : i + 1, :], -1, keepdims=True) for i in range(rows)]
    return jnp.concatenate(parts, axis=0)


def pack_kernel(rows, cols, *refs):
    sources, outs, (tokens_ref, cot_ref, land_ref, vec_ref, perm_ref, sems) = refs[:5], refs[5:-6], refs[-6:]
    copies = [
        pltpu.make_async_copy(source, target, sems.at[n])
        for n, (source, target) in enumerate(zip(sources, (tokens_ref, cot_ref, land_ref, vec_ref, perm_ref)))
    ]
    for copy in copies:
        copy.start()
    for copy in copies:
        copy.wait()
    column = land_column(land_ref, rows, cols)
    added = column * vec_ref[...]
    added = jnp.concatenate([added] * Z, axis=0)
    embedded = (tokens_ref[...].astype(f32) + added).astype(bf16)
    perm = one_hot(perm_ref)
    column = jnp.concatenate([column] * Z, axis=0)
    spare = jnp.broadcast_to(column, (column.shape[0], 2 * 128 - C)).astype(bf16)
    left = mm(perm, jnp.concatenate([embedded, spare], axis=1))
    left, flags = left[:, :C], left[:, C : C + 1]
    right = mm(perm, cot_ref[...])
    packed = jnp.concatenate([left, right], axis=1)
    start = 0
    for out in outs:
        count = out.shape[0] - EXTRA
        eye = lax.broadcasted_iota(jnp.int32, (count, count), 0) == lax.broadcasted_iota(jnp.int32, (count, count), 1)
        row = jnp.sum(jnp.where(eye, flags[start : start + count], 0.0), 0, keepdims=True)
        row = jnp.concatenate([row, jnp.zeros((1, 2 * C - count), f32)], axis=1)
        row = jnp.broadcast_to(row, (EXTRA, 2 * C))
        out[...] = jnp.concatenate([packed[start : start + count], row], axis=0).astype(bf16)
        start += count


def pack(tokens, cotangent, land_sea, vector, rows, cols):
    parts = piece_rows(rows, cols)
    perm = spots(np.concatenate(parts))
    count = Z * rows * cols
    return pl.pallas_call(
        functools.partial(pack_kernel, rows, cols),
        out_shape=[shape((part.size + EXTRA, 2 * C), bf16) for part in parts],
        in_specs=[pl.BlockSpec(memory_space=pltpu.HBM)] * 5,
        out_specs=vmem(4),
        scratch_shapes=[
            pltpu.VMEM((count, C), bf16),
            pltpu.VMEM((count, C), bf16),
            pltpu.VMEM((rows, cols), jnp.int32),
            pltpu.VMEM((1, C), f32),
            pltpu.VMEM((1, count), jnp.int32),
            pltpu.SemaphoreType.DMA((5,)),
        ],
        cost_estimate=cost(4 * count * count * C, 4 * MIB),
        name="pack",
    )(tokens.reshape(count, C), cotangent.reshape(count, C), land_sea, vector.reshape(1, C), perm)


def floor_div(values, divisor):
    return (values * (65536 // divisor + 1)) >> 16


def remainder(values, divisor):
    return values - floor_div(values, divisor) * divisor


def place_order(order):
    half = floor_div(order, SPOTS)
    spot = order - half * SPOTS
    level = floor_div(spot, HH)
    return level * WH + half * HH + (spot - level * HH)


def bias_kernel(levels, table_ref, out_ref, *wide_refs):
    groups = levels * HEADS
    pairs = PLACES * PLACES
    row = lax.broadcasted_iota(jnp.int32, (HEADS * RELW, HEADS * STRIP), 0)
    lane = lax.broadcasted_iota(jnp.int32, (HEADS * RELW, HEADS * STRIP), 1)
    head = floor_div(row, RELW)
    ahead = lane - (head * STRIP + (RELW - 1 - (row - head * RELW)) * SPOTS)
    onehot = ((ahead >= 0) & (ahead < SPOTS)).astype(f32).astype(bf16)
    row = lax.broadcasted_iota(jnp.int32, (pairs, pairs), 0)
    source = place_order(floor_div(row, PLACES)) * PLACES + remainder(row, PLACES)
    reorder = (lax.broadcasted_iota(jnp.int32, (pairs, pairs), 1) == source).astype(f32).astype(bf16)
    for level in range(levels):
        table = table_ref[:, level, :].T
        high = table.astype(bf16)
        rest = (table - high.astype(f32)).astype(bf16)
        wide = mm(mm(reorder, high).astype(bf16), onehot) + mm(mm(reorder, rest).astype(bf16), onehot)
        for head in range(HEADS):
            for n, wide_ref in enumerate(wide_refs):
                start = head * STRIP + n * 128
                wide_ref[(level * HEADS + head) * pairs : (level * HEADS + head + 1) * pairs, :] = wide[:, start : start + 128]
    strips = groups * PLACES
    row = lax.broadcasted_iota(jnp.int32, (strips, STRIP), 0)
    spot = remainder(lax.broadcasted_iota(jnp.int32, (strips, STRIP), 1), SPOTS)
    own = remainder(row, PLACES)
    first_level = (row < HEADS * PLACES).astype(jnp.int32)
    own_north = (own < SPOTS).astype(jnp.int32)
    own_low = (own - SPOTS * (1 - own_north) < HZ * HH).astype(jnp.int32)
    low = (spot < HZ * HH).astype(jnp.int32)
    pole = (lax.axis_index("y") + lax.axis_index("core") == 0).astype(jnp.int32)
    halves = []
    for half in range(2):
        parts = []
        for n, wide_ref in enumerate(wide_refs):
            here = spot[:, n * 128 : (n + 1) * 128]
            part = jnp.zeros((strips, 128), f32)
            for p in range(SPOTS):
                place = p // HH * WH + half * HH + p % HH
                part = jnp.where(here == p, wide_ref[pl.ds(place, strips, stride=PLACES), :], part)
            parts.append(part)
        strip = jnp.concatenate(parts, axis=1)
        differs = first_level * (own_low ^ low) + pole * (own_north ^ (1 - half))
        halves.append(jnp.where(differs > 0, strip + mask_fill, strip) * log2e)
    for w in range(WW):
        start = (WW - 1 - w) * SPOTS
        part = jnp.concatenate([strip[:, start : start + RUN] for strip in halves], axis=1)
        for g in range(groups):
            for half in range(2):
                rows = part[g * PLACES + half * SPOTS : g * PLACES + (half + 1) * SPOTS, :]
                out_ref[g, half * RUN + w * SPOTS : half * RUN + (w + 1) * SPOTS, :] = rows


def expand_bias(table):
    levels = table.shape[1]
    groups = levels * HEADS
    pairs = PLACES * PLACES
    flat = table[0].transpose(1, 3, 0, 2).reshape(HEADS * RELW, levels, pairs)
    return pl.pallas_call(
        functools.partial(bias_kernel, levels),
        out_shape=shape((groups, TOK, TOK), f32),
        in_specs=vmem(1),
        out_specs=vmem(1)[0],
        scratch_shapes=[pltpu.VMEM((groups * pairs, 128), f32)] * (STRIP // 128),
        compiler_params=pltpu.CompilerParams(vmem_limit_bytes=28 * MIB),
        cost_estimate=cost(10**9, 8 * MIB),
        name="bias",
    )(flat)


def head_masks(count):
    lane = lax.broadcasted_iota(jnp.int32, (count, C), 1)
    return [((lane >= h * HEAD) & (lane < (h + 1) * HEAD)).astype(f32) for h in range(HEADS)]


def stacked(values, masks):
    return jnp.concatenate([values * mask for mask in masks], axis=0)


def head_sum(values, masks):
    total = values[:TOK] * masks[0]
    for h in range(1, HEADS):
        total = total + values[h * TOK : (h + 1) * TOK] * masks[h]
    return total


def position():
    return lax.axis_index("core"), lax.axis_index("y") * 2 + lax.axis_index("x"), lax.axis_index("deep")


def chunk_rows(block):
    return pl.ds(pl.multiple_of(block * PART, PART), PART)


def split_parts(total_refs, keep_ref, send_ref):
    core, chip, _ = position()
    for out, side in ((keep_ref, core), (send_ref, 1 - core)):
        parts = []
        for g in range(QUADS):
            rows = chunk_rows(side * QUADS + jnp.bitwise_xor(chip, g))
            parts += [ref[rows, :] for ref in total_refs]
        out[...] = jnp.concatenate(parts, axis=0).astype(out.dtype)


def attend(first, runs, pieces, bias_ref, triple_ref, project_ref, *refs):
    q_ref, k_ref, v_ref, p_ref, mixed_ref, normed_ref, unit_ref, spread_ref, summed_ref, cot_ref = refs
    pieces = [piece.astype(f32) for piece in pieces]
    ordered = jnp.concatenate([pieces[n][start : start + count] for n, start, count in runs], axis=0)
    emb = ordered[:, :C]
    cot_ref[...] = ordered[:, C:].astype(bf16)
    unit, spread = unit_norm(emb)
    unit_ref[...] = unit
    spread_ref[...] = spread
    normed = unit.astype(bf16)
    normed_ref[...] = normed
    packed = mm(normed, triple_ref[...])
    q_ref[...] = packed[:, :C].astype(bf16)
    k_ref[...] = packed[:, C : 2 * C].astype(bf16)
    v_ref[...] = packed[:, 2 * C :].astype(bf16)
    masks = head_masks(TOK)
    masks_b = [mask.astype(bf16) for mask in masks]
    for w in range(emb.shape[0] // TOK):
        rows = slice(w * TOK, (w + 1) * TOK)
        heads = slice(w * HEADS, (w + 1) * HEADS)
        level = (first + w) % (Z // WZ)
        scores = mm_nt(stacked(q_ref[rows, :], masks_b), k_ref[rows, :])
        bias = bias_ref[level * HEADS : (level + 1) * HEADS].reshape(HEADS * TOK, TOK)
        raised = jnp.exp2(scores * (score_scale * log2e) + bias)
        probs = raised * (1.0 / jnp.sum(raised, -1, keepdims=True))
        probs_b = probs.astype(bf16)
        p_ref[heads] = probs_b.reshape(HEADS, TOK, TOK)
        mixed = head_sum(mm(probs_b, v_ref[rows, :]), masks).astype(bf16)
        mixed_ref[rows, :] = mixed
        summed_ref[rows, :] = emb[rows] + mm(mixed, project_ref[...]).astype(bf16).astype(f32)


def feed_back(summed, cot, up_ref, down_ref, gsum_ref, up_grad_ref, down_grad_ref):
    unit2, spread2 = unit_norm(summed)
    normed2 = unit2.astype(bf16)
    back = jnp.zeros(unit2.shape, f32)
    block = 256
    for start in range(0, FF, block):
        cols = slice(start, start + block)
        up_part = up_ref[:, cols]
        pre = mm(normed2, up_part)
        upstream = mm(cot, down_ref[:, cols])
        phi = 0.5 * (1.0 + lax.erf(pre * root_half))
        activated = (pre * phi).astype(bf16)
        slope = phi + pre * inv_root_tau * jnp.exp2(pre * pre * (-0.5 * log2e))
        hidden = (upstream * slope).astype(bf16)
        up_grad_ref[:, cols] = mm_tn(normed2, hidden)
        down_grad_ref[:, cols] = mm_tn(cot, activated)
        back = back + mm_nt(hidden, up_part)
    gsum_ref[...] = cot.astype(f32) + norm_back(back, unit2, spread2)


def attend_back(at, q_ref, k_ref, v_ref, p_ref, gsum_ref, project_ref, gq_ref, gk_ref, gv_ref):
    masks = head_masks(TOK)
    masks_b = [mask.astype(bf16) for mask in masks]
    for w in range(q_ref.shape[0] // TOK):
        rows = slice(w * TOK, (w + 1) * TOK)
        full_rows = slice(at + w * TOK, at + (w + 1) * TOK)
        grad = gsum_ref[full_rows, :].astype(bf16)
        grad_mixed_b = mm_nt(grad, project_ref[...]).astype(bf16)
        probs_b = p_ref[w * HEADS : (w + 1) * HEADS].reshape(HEADS * TOK, TOK)
        probs = probs_b.astype(f32)
        grad_probs = mm_nt(stacked(grad_mixed_b, masks_b), v_ref[rows, :])
        inner = jnp.sum(grad_probs * probs, -1, keepdims=True)
        scaled = (probs * (grad_probs - inner) * score_scale).astype(bf16)
        grad_q = head_sum(mm(scaled, k_ref[rows, :]), masks)
        grad_mixed_t = grad_mixed_b.astype(f32).T.astype(bf16)
        query_t = q_ref[rows, :].astype(f32).T.astype(bf16)
        grad_k, grad_v = [], []
        for h in range(HEADS):
            spot = slice(h * HEAD, (h + 1) * HEAD)
            span = slice(h * TOK, (h + 1) * TOK)
            grad_k.append(mm(query_t[spot], scaled[span]))
            grad_v.append(mm(grad_mixed_t[spot], probs_b[span]))
        gq_ref[full_rows, :] = grad_q.astype(bf16)
        gk_ref[full_rows, :] = jnp.concatenate(grad_k, axis=0).T.astype(bf16)
        gv_ref[full_rows, :] = jnp.concatenate(grad_v, axis=0).T.astype(bf16)


def halved(rows):
    return -(-rows // 16) * 8


def tokens_back(
    lon_windows, sizes, gq_ref, gk_ref, gv_ref, mixed, normed, unit, spread, gsum_ref, triple_ref, up_grad_ref, down_grad_ref,
    *rest,
):
    flag_refs, rest = rest[: len(sizes)], rest[len(sizes) :]
    outs, (land_ref, keep_ref, send_ref, total_ref) = rest[: len(sizes) - 1], rest[len(sizes) - 1 :]
    triple = triple_ref[...]
    grad_normed = jnp.zeros(unit.shape, f32)
    parts = []
    for n, ref in enumerate((gq_ref, gk_ref, gv_ref)):
        grad = ref[...]
        grad_normed = grad_normed + mm_nt(grad, triple[:, n * C : (n + 1) * C])
        parts.append(mm_tn(normed, grad))
    parts.append(mm_tn(mixed, gsum_ref[...].astype(bf16)))
    total_ref[...] = jnp.concatenate(parts, axis=1)
    grad_normed = grad_normed.astype(bf16).astype(f32)
    grad_tokens = gsum_ref[...] + norm_back(grad_normed, unit, spread)
    parts, at = [[] for _ in sizes], 0
    for n, start, count in [run for window in window_runs(lon_windows) for run in window]:
        parts[n].append((start, grad_tokens[at : at + count]))
        at += count
    land = jnp.zeros((EXTRA, C), f32)
    wide = []
    for size, flag_ref, part in zip(sizes, flag_refs, parts):
        piece = jnp.concatenate([value for _, value in sorted(part, key=lambda item: item[0])], axis=0)
        flags = flag_ref[size - 8 : size + 8, :].astype(f32)[8:, :size]
        land = land + mm(flags.astype(bf16), piece.astype(bf16))
        half = halved(size)
        second = jnp.concatenate([piece[half:], jnp.zeros((2 * half - size, C), f32)], axis=0)
        wide.append(jnp.concatenate([piece[:half], second], axis=1))
    land_ref[...] = land[0:1]
    own, north, side, corner = wide
    for out, value in zip(outs, (own, jnp.concatenate([north, corner], axis=0), side)):
        out[...] = value.astype(bf16)
    split_parts((up_grad_ref, down_grad_ref, total_ref), keep_ref, send_ref)


def saved_shapes(count):
    dims = [((count, C), bf16)] * 3 + [((count // TOK * HEADS, TOK, TOK), bf16)] + [((count, C), bf16)] * 2
    return dims + [((count, C), f32), ((count, 1), f32), ((count, C), f32), ((count, C), bf16)]


SAVED = len(saved_shapes(TOK))


def split_runs(lon_windows):
    windows = window_runs(lon_windows)
    whole = (lon_windows - 1) * (Z // WZ)
    return whole, *[[run for window in part for run in window] for part in (windows[:whole], windows[whole:])]


def near_kernel(lon_windows, own_ref, north_ref, *refs):
    runs = split_runs(lon_windows)[1]
    attend(0, runs, (own_ref[...], north_ref[...]), *refs)


def near_block(own, north, bias, triple, project, lon_windows):
    count = split_runs(lon_windows)[0] * TOK
    return pl.pallas_call(
        functools.partial(near_kernel, lon_windows),
        out_shape=[shape(*dims) for dims in saved_shapes(count)],
        in_specs=vmem(5),
        out_specs=vmem(SAVED),
        compiler_params=pltpu.CompilerParams(vmem_limit_bytes=24 * MIB),
        cost_estimate=cost(3 * 10**9, 8 * MIB),
        name="near_block",
    )(own, north, bias, triple, project)


def block_kernel(lon_windows, sizes, *refs):
    whole, _, runs = split_runs(lon_windows)
    pieces, refs = refs[:4], refs[4:]
    (bias_ref, triple_ref, project_ref, up_ref, down_ref), refs = refs[:5], refs[5:]
    near, refs = refs[:SAVED], refs[SAVED:]
    outs, refs = refs[: len(sizes) + 2], refs[len(sizes) + 2 :]
    far, (gsum, up_grad, down_grad, gq, gk, gv, total) = refs[:SAVED], refs[SAVED:]
    attend(whole, runs, [ref[...] for ref in pieces], bias_ref, triple_ref, project_ref, *far)
    mixed, normed, unit, spread, summed, cot = [
        jnp.concatenate([one[...], other[...]], axis=0) for one, other in zip(near[4:], far[4:])
    ]
    feed_back(summed, cot, up_ref, down_ref, gsum, up_grad, down_grad)
    attend_back(0, *near[:4], gsum, project_ref, gq, gk, gv)
    attend_back(whole * TOK, *far[:4], gsum, project_ref, gq, gk, gv)
    tokens_back(
        lon_windows, sizes, gq, gk, gv, mixed, normed, unit, spread, gsum, triple_ref, up_grad, down_grad,
        *pieces, *outs, total,
    )


def block(pieces, bias, triple, project, up, down, near, lon_windows, sizes):
    count = sum(sizes)
    own, north, side, corner = [halved(size) for size in sizes]
    out_shape = [shape((size, 2 * C), bf16) for size in (own, north + corner, side)] + [
        shape((1, C), f32),
        shape((QUADS * CHUNK, FF), f32),
        shape((QUADS * CHUNK, FF), bf16),
    ]
    return pl.pallas_call(
        functools.partial(block_kernel, lon_windows, sizes),
        out_shape=out_shape,
        in_specs=vmem(9 + SAVED),
        out_specs=vmem(len(out_shape)),
        scratch_shapes=[pltpu.VMEM(*dims) for dims in saved_shapes(count - near[0].shape[0])]
        + [pltpu.VMEM((count, C), f32)]
        + [pltpu.VMEM((C, FF), f32)] * 2
        + [pltpu.VMEM((count, C), bf16)] * 3
        + [pltpu.VMEM((C, FF), f32)],
        compiler_params=pltpu.CompilerParams(vmem_limit_bytes=28 * MIB),
        cost_estimate=cost(8 * 10**9, 16 * MIB),
        name="block",
    )(*pieces, bias, triple, project, up, down, *near)


def side_kernel(side_ref, north_ref, *refs):
    corner = north_ref[...].astype(f32)[-side_ref.shape[0] :]
    refs[-1][...] = jnp.concatenate([side_ref[...].astype(f32), corner], axis=0).astype(bf16)


def home_kernel(sizes, own_ref, north_ref, side_ref, perm_ref, out_ref):
    wide = [ref[...].astype(f32) for ref in (own_ref, north_ref, side_ref)]
    half = wide[2].shape[0] // 2
    wide = [wide[0], wide[1][:-half], wide[2][:half], wide[2][half:]]
    pieces = []
    for size, value in zip(sizes, wide):
        pieces += [value[:, :C], value[: size - value.shape[0], C:]]
    pieces = jnp.concatenate(pieces, axis=0).astype(bf16)
    out_ref[...] = mm(one_hot(perm_ref), pieces).astype(bf16)


def to_home(own, north, side, sizes, rows, cols):
    count = Z * rows * cols
    perm = spots(np.argsort(np.concatenate(piece_rows(rows, cols))))
    return pl.pallas_call(
        functools.partial(home_kernel, sizes),
        out_shape=shape((count, C), bf16),
        in_specs=vmem(4),
        out_specs=vmem(1)[0],
        compiler_params=pltpu.CompilerParams(vmem_limit_bytes=32 * MIB),
        cost_estimate=cost(2 * count * count * C, 4 * MIB),
        name="to_home",
    )(own, north, side, perm)


def core_add_kernel(keep_ref, got_ref, *refs):
    own_ref, outs = refs[-QUADS], refs[1 - QUADS :]
    total = keep_ref[...] + got_ref[...].astype(f32)
    own_ref[...] = total[:CHUNK]
    for e, out in zip(FAR_FIRST, outs):
        out[...] = total[e * CHUNK : (e + 1) * CHUNK].astype(bf16)


def chip_add_kernel(keep_ref, *refs):
    gots, (land_ref, out_ref) = refs[:-2], refs[-2:]
    total = keep_ref[...]
    for ref in gots:
        total = total + ref[...].astype(f32)
    land = land_ref[...]
    rest = jnp.concatenate([land[:, 128:], jnp.zeros((1, 2 * 128 - C), f32)], axis=1)
    parts = [total[:, n * 128 : (n + 1) * 128] for n in range(BLOCKS)]
    total = jnp.concatenate(parts + [land[:, :128], rest, jnp.zeros((EXTRA - 2, 128), f32)], axis=0)
    out_ref[...] = total.astype(bf16)


def add_kernel(one_ref, two_ref, *refs):
    refs[-1][...] = (one_ref[...].astype(f32) + two_ref[...].astype(f32)).astype(bf16)


def join_kernel(*refs):
    refs[-1][...] = jnp.concatenate([ref[...] for ref in refs[:-1]], axis=0)


def small_call(kernel, out_shape, args, name, after=(), scratch=()):
    return pl.pallas_call(
        kernel,
        out_shape=out_shape,
        in_specs=vmem(len(args)) + [pl.BlockSpec(memory_space=pl.ANY)] * len(after),
        out_specs=vmem(len(out_shape)),
        scratch_shapes=scratch,
        compiler_params=pltpu.CompilerParams(vmem_limit_bytes=16 * MIB),
        cost_estimate=cost(10**6, 2 * MIB),
        name=name,
    )(*args, *after)


def finish_kernel(far, chunks_ref, *refs):
    if far:
        before_ref, refs = refs[0], refs[5:]
    outs, land_ref, (up_ref, down_ref, triple_ref, project_ref, lands_ref, sum_ref, sems) = refs[:4], refs[4], refs[5:]
    core, chip, _ = position()
    side = 1 - core if far else core
    for g in range(QUADS):
        tiles = chunks_ref[g * FULL : (g + 1) * FULL, :].astype(f32)
        chunk = jnp.concatenate([tiles[n * CHUNK : (n + 1) * CHUNK] for n in range(BLOCKS)], axis=1)
        block = jnp.bitwise_xor(chip, g)
        rows = chunk_rows(block)
        up_ref[rows, :] = chunk[:PART]
        down_ref[rows, :] = chunk[PART : 2 * PART]
        triple_ref[rows, :] = chunk[2 * PART : CHUNK, : 3 * C]
        project_ref[rows, :] = chunk[2 * PART : CHUNK, 3 * C :]
        lands_ref[pl.ds(pl.multiple_of(block * EXTRA, EXTRA), EXTRA), :] = tiles[BLOCKS * CHUNK :]
    copies = []
    for n, (source, out) in enumerate(zip((triple_ref, project_ref, up_ref, down_ref), outs)):
        rows = pl.ds(pl.multiple_of(side * QUADS * PART, 8), QUADS * PART)
        copies.append(pltpu.make_async_copy(source, out.at[rows, :], sems.at[n]))
    for copy in copies:
        copy.start()
    lands = lands_ref[...]
    lands = [sum(lands[g * EXTRA + n : g * EXTRA + n + 1] for g in range(QUADS)) for n in range(2)]
    land = jnp.concatenate([lands[0], lands[1][:, : C - 128]], axis=1)
    if far:
        sum_ref[...] = land + before_ref[...]
        copies.append(pltpu.make_async_copy(sum_ref, land_ref, sems.at[4]))
        copies[-1].start()
    else:
        land_ref[...] = land
    for copy in copies:
        copy.wait()


def finish(chunks, before=()):
    rows = QUADS * PART
    widths = (3 * C, C, FF, FF)
    hbm = [pl.BlockSpec(memory_space=pltpu.HBM)] * 4
    land, weights = before[4:], before[:4]
    return pl.pallas_call(
        functools.partial(finish_kernel, bool(before)),
        out_shape=[shape((C, width), f32) for width in widths] + [shape((1, C), f32)],
        in_specs=vmem(1 + len(land)) + hbm[: len(weights)],
        out_specs=hbm + (hbm[:1] if before else vmem(1)),
        scratch_shapes=[
            pltpu.VMEM((rows, FF), f32),
            pltpu.VMEM((rows, FF), f32),
            pltpu.VMEM((rows, 3 * C), f32),
            pltpu.VMEM((rows, C), f32),
            pltpu.VMEM((QUADS * EXTRA, 128), f32),
            pltpu.VMEM((1, C), f32),
            pltpu.SemaphoreType.DMA((5,)),
        ],
        input_output_aliases={2 + n: n for n in range(len(weights))},
        compiler_params=pltpu.CompilerParams(vmem_limit_bytes=16 * MIB),
        cost_estimate=cost(10**6, 2 * MIB),
        name="finish_far" if before else "finish_own",
    )(chunks, *land, *weights)


def reduce_all(keep, sent, land, side, north, go_home, shift, lon_count):
    core_move = lambda lon, lat: (lon, lat ^ 1)
    chip_move = lambda e: lambda lon, lat: (lon ^ (e & 1), lat ^ (2 * (e >> 1)))
    deep_move = lambda e: lambda lon, lat: (lon ^ (2 * e), lat)

    def one(rows):
        return [shape((rows, FF), bf16)]

    got = shift(sent, move=core_move)
    parts = [shape((CHUNK, FF), f32)] + one(CHUNK) * (QUADS - 1)
    own, *parts = small_call(core_add_kernel, parts, (keep, got), "core_add", after=(north,))
    gots = [shift(value, move=chip_move(e)) for e, value in zip(FAR_FIRST, parts)]
    full = [shape((FULL, 128), bf16)]
    (total,) = small_call(chip_add_kernel, full, (own, *gots, land), "chip_add")
    (side,) = small_call(side_kernel, [shape((2 * side.shape[0], 2 * C), bf16)], (side, north), "side", after=(total,))
    side = shift(side, move=lambda lon, lat: (lon - 1, lat))
    grad_tokens = go_home(north, side)
    reach, waits = 1, [(side,), (grad_tokens,)]
    while reach < lon_count // 2:
        got = shift(total, move=deep_move(reach))
        reach *= 2
        (total,) = small_call(add_kernel, full, (total, got), "deep_add", after=waits.pop(0) if waits else ())
    near = [total] + [shift(total, move=chip_move(e)) for e in range(1, QUADS)]
    (total,) = small_call(join_kernel, [shape((QUADS * FULL, 128), bf16)], near, "join")
    got = shift(total, move=core_move)
    return finish(got, finish(total)), grad_tokens


AXES = ("deep", "x", "y", "core")


def send(value, lon_count, lat_count, move):
    pairs = []
    for lon in range(lon_count):
        for lat in range(lat_count):
            to_lon, to_lat = move(lon, lat)
            pairs.append((lon * lat_count + lat, (to_lon % lon_count) * lat_count + to_lat % lat_count))
    return lax.ppermute(value, AXES, pairs)


def body(
    lon_count, lat_count,
    tokens, cotangent, land_sea, land_vector, triple_weight, project_weight, up_weight, down_weight, earth_bias,
):
    levels, rows, cols, features = tokens.shape
    shift = functools.partial(send, lon_count=lon_count, lat_count=lat_count)
    lon_windows = cols // WW

    own, north, side, corner = pack(tokens, cotangent, land_sea, land_vector, rows, cols)
    north = shift(north, move=lambda lon, lat: (lon, lat + 1))
    side = shift(side, move=lambda lon, lat: (lon + 1, lat))
    corner = shift(corner, move=lambda lon, lat: (lon + 1, lat + 1))
    bias = expand_bias(earth_bias)

    sizes = [part.size for part in piece_rows(rows, cols)]
    pieces = (own, north, side, corner)
    near = near_block(own, north, bias, triple_weight, project_weight, lon_windows)
    own, north, side, land, keep, sent = block(
        pieces, bias, triple_weight, project_weight, up_weight, down_weight.T, near, lon_windows, sizes
    )
    north = shift(north, move=lambda lon, lat: (lon, lat - 1))
    go_home = lambda north, side: to_home(own, north, side, sizes, rows, cols)
    sums, grad_tokens = reduce_all(keep, sent, land, side, north, go_home, shift, lon_count)
    triple, project, up, down, land = sums
    return grad_tokens.reshape(tokens.shape), triple, project, up, down.T, land.reshape(features)


def solution(mesh):
    lon_count, lat_count = mesh.shape["lon"], mesh.shape["lat"]
    fine = jax.sharding.Mesh(mesh.devices.reshape(lon_count // 2, 2, lat_count // 2, 2), AXES)
    lon, lat = AXES[:2], AXES[2:]
    return jax.shard_map(
        functools.partial(body, lon_count, lat_count),
        mesh=fine,
        in_specs=(
            P(None, lat, lon, None),
            P(None, lat, lon, None),
            P(lat, lon),
            P(),
            P(),
            P(),
            P(),
            P(),
            P(lat, None, None, None, None),
        ),
        out_specs=(P(None, lat, lon, None), P(), P(), P(), P(), P()),
        check_vma=False,
    )
```

profile of v0, /device:TPU:0, one launch (start us, length us, event | category | flops | bytes accessed | tf_op | source)
XLA Modules:
  0.0 60.0 jit_solution(806685982670628258)
XLA Ops:
  0.6 2.7 %pack.1 = (bf16[224,384]{1,0:T(8,128)(2,1)}, bf16[224,384]{1,0:T(8,128)(2,1)}, bf16[80,384]{1,0:T(8,128)(2,1)}, bf16[80,384]{1,0:T(8,128)(2,1)}) custom-call(bf16[576,192]{1,0:T(8,128)(2,1)} %bitcast.16, bf16[576,192]{1,0:T(8,128)(2,1)} %bitcast.17, s32[6,24]{1,0:T(8,128)} %refs_2_.2, f32[1,192]{1,0:T(1,128)} %bitcast.18, s32[1,576]{1,0:T(1,128)} %constant.4.clone.refs_4_), custom_call_target="tpu_custom_call" | custom-call | flops 254803968 | bytes 4194304 | tf_op jit(solution)/shard_map/pack/pallas_call | solution.py:170
  3.3 0.5 collective-permute-start
  3.8 2.6 %collective-permute-start.1 = (bf16[80,384]{1,0:T(8,128)(2,1)}, bf16[80,384]{1,0:T(8,128)(2,1)S(1)}, u32[]{:S(2)}, u32[]{:S(2)}) collective-permute-start(bf16[80,384]{1,0:T(8,128)(2,1)} %get-tuple-element.42), channel_id=1, source_target_pairs={{0,4},{1,5},{2,6},{3,7},{4,8},{5,9},{6,10},{7,11},{8,12},{9,13},{1... | collective-permute-start | bytes 184328 | tf_op jit(solution)/shard_map/ppermute | solution.py:670
  6.4 2.4 %collective-permute-start.2 = (bf16[80,384]{1,0:T(8,128)(2,1)}, bf16[80,384]{1,0:T(8,128)(2,1)S(1)}, u32[]{:S(2)}, u32[]{:S(2)}) collective-permute-start(bf16[80,384]{1,0:T(8,128)(2,1)} %get-tuple-element.43), channel_id=1, source_target_pairs={{0,5},{1,6},{2,7},{3,4},{4,9},{5,10},{6,11},{7,8},{8,13},{9,14},{1... | collective-permute-start | bytes 184328 | tf_op jit(solution)/shard_map/ppermute | solution.py:670
  8.8 0.0 copy-start.4
  8.8 1.0 %copy-done.4 = f32[1,2,6,144,23]{3,1,4,2,0:T(2,128)S(1)} copy-done((f32[1,2,6,144,23]{3,1,4,2,0:T(2,128)S(1)}, f32[1,2,6,144,23]{3,1,4,2,0:T(2,128)}, u32[]{:S(2)}) %copy-start.4) | copy-done | bytes 159000
  9.8 0.0 copy-start.5
  9.8 0.0 copy-start.6
  9.8 0.0 copy-start.7
  9.8 1.4 %bias.1.refs_0_.refs_4_ = f32[12,144,144]{2,1,0:T(8,128)S(1)} custom-call(f32[138,2,144]{2,1,0:T(2,128)S(1)} %bitcast.14), custom_call_target="tpu_custom_call" | custom-call | flops 1000000000 | bytes 8388608 | tf_op jit(solution)/shard_map/bias/pallas_call | solution.py:259
  11.2 0.0 collective-permute-done.north_ref.refs_1_
  11.2 0.0 copy-done.5
  11.2 0.0 copy-done.6
  11.2 0.0 copy-done.7
  11.2 0.0 copy-start.2
  11.2 0.0 copy-start.3
  11.3 1.8 %near_block.1 = (bf16[288,192]{1,0:T(8,128)(2,1)S(1)}, bf16[288,192]{1,0:T(8,128)(2,1)S(1)}, bf16[288,192]{1,0:T(8,128)(2,1)S(1)}, bf16[12,144,144]{2,1,0:T(8,12...) custom-call(bf16[224,384]{1,0:T(8,128)(2,1)S(1)} %copy-done.7, ...), custom_call_target="tpu_custom_call" | custom-call | flops 3000000000 | bytes 8388608 | tf_op jit(solution)/shard_map/near_block/pallas_call | solution.py:446
  13.1 0.0 collective-permute-done.1.refs_2_
  13.1 1.2 %collective-permute-done.2.refs_3_ = bf16[80,384]{1,0:T(8,128)(2,1)S(1)} collective-permute-done((bf16[80,384]{1,0:T(8,128)(2,1)}, bf16[80,384]{1,0:T(8,128)(2,1)S(1)}, u32[]{:S(2)}, u32[]{:S(2)}) %collective-permute-start.2) | collective-permute-done | bytes 61472 | tf_op jit(solution)/shard_map/ppermute | solution.py:670
  14.3 0.0 copy-done.2
  14.3 0.0 copy-done.3
  14.3 7.6 %block.1 = (bf16[112,384]{1,0:T(8,128)(2,1)S(1)}, bf16[152,384]{1,0:T(8,128)(2,1)S(1)}, bf16[40,384]{1,0:T(8,128)(2,1)S(1)}, f32[1,192]{1,0:T(1,128)S(1)}, f32[2...) custom-call(bf16[224,384]{1,0:T(8,128)(2,1)S(1)} %copy-done.7, ...), custom_call_target="tpu_custom_call" | custom-call | flops 8000000000 | bytes 16777216 | tf_op jit(solution)/shard_map/block/pallas_call | solution.py:485
  21.9 0.0 copy-start.1
  21.9 0.2 collective-permute-start.4
  22.1 1.2 %collective-permute-start.3 = (bf16[152,384]{1,0:T(8,128)(2,1)S(1)}, bf16[152,384]{1,0:T(8,128)(2,1)S(1)}, u32[]{:S(2)}, u32[]{:S(2)}) collective-permute-start(bf16[152,384]{1,0:T(8,128)(2,1)S(1)} %get-tuple-element.55), channel_id=1, source_target_pairs={{0,3},{1,0},{2,1},{3,2},{4,7},{5,4},{6,5},{7,6},{8,11},{9,8},{10,9... | collective-permute-start | bytes 350216 | tf_op jit(solution)/shard_map/ppermute | solution.py:670
  23.3 2.4 %collective-permute-done.3.refs_0_.north_ref = bf16[152,384]{1,0:T(8,128)(2,1)S(1)} collective-permute-done((bf16[152,384]{1,0:T(8,128)(2,1)S(1)}, bf16[152,384]{1,0:T(8,128)(2,1)S(1)}, u32[]{:S(2)}, u32[]{:S(2)}) %collective-permute-start.3) | collective-permute-done | bytes 116768 | tf_op jit(solution)/shard_map/ppermute | solution.py:670
  25.7 0.0 collective-permute-done.4.got_ref
  25.7 0.1 core_add.1
  25.8 0.6 collective-permute-start.5
  26.4 0.5 collective-permute-start.6
  26.9 2.5 %collective-permute-start.7 = (bf16[72,768]{1,0:T(8,128)(2,1)S(1)}, bf16[72,768]{1,0:T(8,128)(2,1)S(1)}, u32[]{:S(2)}, u32[]{:S(2)}) collective-permute-start(bf16[72,768]{1,0:T(8,128)(2,1)S(1)} %get-tuple-element.62), channel_id=1, source_target_pairs={{0,4},{1,5},{2,6},{3,7},{4,0},{5,1},{6,2},{7,3},{8,12},{9,13},{10,... | collective-permute-start | bytes 331784 | tf_op jit(solution)/shard_map/ppermute | solution.py:670
  29.4 3.4 %collective-permute-done.5.refs_0_ = bf16[72,768]{1,0:T(8,128)(2,1)S(1)} collective-permute-done((bf16[72,768]{1,0:T(8,128)(2,1)S(1)}, bf16[72,768]{1,0:T(8,128)(2,1)S(1)}, u32[]{:S(2)}, u32[]{:S(2)}) %collective-permute-start.5) | collective-permute-done | bytes 110624 | tf_op jit(solution)/shard_map/ppermute | solution.py:670
  32.8 1.5 %collective-permute-done.6.refs_1_ = bf16[72,768]{1,0:T(8,128)(2,1)S(1)} collective-permute-done((bf16[72,768]{1,0:T(8,128)(2,1)S(1)}, bf16[72,768]{1,0:T(8,128)(2,1)S(1)}, u32[]{:S(2)}, u32[]{:S(2)}) %collective-permute-start.6) | collective-permute-done | bytes 110624 | tf_op jit(solution)/shard_map/ppermute | solution.py:670
  34.3 0.0 collective-permute-done.7.refs_2_
  34.3 0.1 chip_add.1.refs_0_.one_ref
  34.4 0.6 %collective-permute-start.9 = (bf16[440,128]{1,0:T(8,128)(2,1)S(1)}, bf16[440,128]{1,0:T(8,128)(2,1)S(1)}, u32[]{:S(2)}, u32[]{:S(2)}) collective-permute-start(bf16[440,128]{1,0:T(8,128)(2,1)S(1)} %chip_add.1.refs_0_.one_ref), channel_id=1, source_target_pairs={{0,8},{1,9},{2,10},{3,11},{4,12},{5,13},{6,14},{7,15},{8,0},{9,1},... | collective-permute-start | bytes 337928 | tf_op jit(solution)/shard_map/ppermute | solution.py:670
  35.0 3.3 %collective-permute-start.8 = (bf16[80,384]{1,0:T(8,128)(2,1)S(1)}, bf16[80,384]{1,0:T(8,128)(2,1)S(1)}, u32[]{:S(2)}, u32[]{:S(2)}) collective-permute-start(bf16[80,384]{1,0:T(8,128)(2,1)S(1)} %side.1), channel_id=1, source_target_pairs={{0,28},{1,29},{2,30},{3,31},{4,0},{5,1},{6,2},{7,3},{8,4},{9,5},{1... | collective-permute-start | bytes 184328 | tf_op jit(solution)/shard_map/ppermute | solution.py:670
  38.3 1.9 %collective-permute-done.8.side_ref.refs_0_ = bf16[80,384]{1,0:T(8,128)(2,1)S(1)} collective-permute-done((bf16[80,384]{1,0:T(8,128)(2,1)S(1)}, bf16[80,384]{1,0:T(8,128)(2,1)S(1)}, u32[]{:S(2)}, u32[]{:S(2)}) %collective-permute-start.8) | collective-permute-done | bytes 61472 | tf_op jit(solution)/shard_map/ppermute | solution.py:670
  40.2 0.1 collective-permute-done.9.two_ref
  40.2 1.6 %collective-permute-start.10 = (bf16[440,128]{1,0:T(8,128)(2,1)S(1)}, bf16[440,128]{1,0:T(8,128)(2,1)S(1)}, u32[]{:S(2)}, u32[]{:S(2)}) collective-permute-start(bf16[440,128]{1,0:T(8,128)(2,1)S(1)} %deep_add.2.one_ref), channel_id=1, source_target_pairs={{0,16},{1,17},{2,18},{3,19},{4,20},{5,21},{6,22},{7,23},{8,24},{9,... | collective-permute-start | bytes 337928 | tf_op jit(solution)/shard_map/ppermute | solution.py:670
  41.9 0.0 copy-done.1
  41.9 1.2 %to_home.1.refs_0_ = bf16[576,192]{1,0:T(8,128)(2,1)} custom-call(bf16[112,384]{1,0:T(8,128)(2,1)S(1)} %get-tuple-element.54.own_ref, bf16[152,384]{1,0:T(8,128)(2,1)S(1)} %collective-permute-done.3.refs_0_.north_ref, bf16[80,384]{1,0:T(8,128)(2,1)S(1)} %collective-permute-done.8.side_ref.refs_0_, s32[1,576]{1,0:T(1,128)S(1)} %copy-done.1), custom_call_target="tpu_custom_call" | custom-call | flops 127401984 | bytes 4194304 | tf_op jit(solution)/shard_map/to_home/pallas_call | solution.py:520
  43.1 4.5 %collective-permute-done.10.two_ref = bf16[440,128]{1,0:T(8,128)(2,1)S(1)} collective-permute-done((bf16[440,128]{1,0:T(8,128)(2,1)S(1)}, bf16[440,128]{1,0:T(8,128)(2,1)S(1)}, u32[]{:S(2)}, u32[]{:S(2)}) %collective-permute-start.10) | collective-permute-done | bytes 112672 | tf_op jit(solution)/shard_map/ppermute | solution.py:670
  47.5 0.0 copy-start
  47.5 1.0 %copy-done = bf16[576,192]{1,0:T(8,128)(2,1)S(1)} copy-done((bf16[576,192]{1,0:T(8,128)(2,1)S(1)}, bf16[576,192]{1,0:T(8,128)(2,1)}, u32[]{:S(2)}) %copy-start) | copy-done | bytes 221208
  48.5 3.1 %collective-permute-start.13 = (bf16[440,128]{1,0:T(8,128)(2,1)S(1)}, bf16[440,128]{1,0:T(8,128)(2,1)S(1)}, u32[]{:S(2)}, u32[]{:S(2)}) collective-permute-start(bf16[440,128]{1,0:T(8,128)(2,1)S(1)} %deep_add.3.refs_0_), channel_id=1, source_target_pairs={{0,6},{1,7},{2,4},{3,5},{4,2},{5,3},{6,0},{7,1},{8,14},{9,15},{10,... | collective-permute-start | bytes 337928 | tf_op jit(solution)/shard_map/ppermute | solution.py:670
  51.6 0.6 %collective-permute-start.12 = (bf16[440,128]{1,0:T(8,128)(2,1)S(1)}, bf16[440,128]{1,0:T(8,128)(2,1)S(1)}, u32[]{:S(2)}, u32[]{:S(2)}) collective-permute-start(bf16[440,128]{1,0:T(8,128)(2,1)S(1)} %deep_add.3.refs_0_), channel_id=1, source_target_pairs={{0,2},{1,3},{2,0},{3,1},{4,6},{5,7},{6,4},{7,5},{8,10},{9,11},{10,... | collective-permute-start | bytes 337928 | tf_op jit(solution)/shard_map/ppermute | solution.py:670
  52.3 0.0 collective-permute-start.11
  52.3 2.4 %collective-permute-done.13.refs_3_ = bf16[440,128]{1,0:T(8,128)(2,1)S(1)} collective-permute-done((bf16[440,128]{1,0:T(8,128)(2,1)S(1)}, bf16[440,128]{1,0:T(8,128)(2,1)S(1)}, u32[]{:S(2)}, u32[]{:S(2)}) %collective-permute-start.13) | collective-permute-done | bytes 112672 | tf_op jit(solution)/shard_map/ppermute | solution.py:670
  54.7 2.1 %collective-permute-done.12.refs_2_ = bf16[440,128]{1,0:T(8,128)(2,1)S(1)} collective-permute-done((bf16[440,128]{1,0:T(8,128)(2,1)S(1)}, bf16[440,128]{1,0:T(8,128)(2,1)S(1)}, u32[]{:S(2)}, u32[]{:S(2)}) %collective-permute-start.12) | collective-permute-done | bytes 112672 | tf_op jit(solution)/shard_map/ppermute | solution.py:670
  56.8 0.2 collective-permute-done.11.refs_1_
  57.0 0.1 join.1.chunks_ref
  57.1 0.1 collective-permute-start.14
  57.2 1.0 %finish_own.1 = (f32[192,576]{1,0:T(8,128)}, f32[192,192]{1,0:T(8,128)}, f32[192,768]{1,0:T(8,128)}, f32[192,768]{1,0:T(8,128)}, f32[1,192]{1,0:T(1,128)S(1)}) custom-call(bf16[1760,128]{1,0:T(8,128)(2,1)S(1)} %join.1.chunks_ref), custom_call_target="tpu_custom_call" | custom-call | flops 1000000 | bytes 2097152 | tf_op jit(solution)/shard_map/finish_own/pallas_call | solution.py:612
  58.2 0.7 %collective-permute-done.14.chunks_ref = bf16[1760,128]{1,0:T(8,128)(2,1)S(1)} collective-permute-done((bf16[1760,128]{1,0:T(8,128)(2,1)S(1)}, bf16[1760,128]{1,0:T(8,128)(2,1)S(1)}, u32[]{:S(2)}, u32[]{:S(2)}) %collective-permute-start.14) | collective-permute-done | bytes 450592 | tf_op jit(solution)/shard_map/ppermute | solution.py:670
  59.0 1.0 %finish_far.1 = (f32[192,576]{1,0:T(8,128)}, f32[192,192]{1,0:T(8,128)}, f32[192,768]{1,0:T(8,128)}, f32[192,768]{1,0:T(8,128)}, f32[1,192]{1,0:T(1,128)}) custom-call(bf16[1760,128]{1,0:T(8,128)(2,1)S(1)} %collective-permute-done.14.chunks_ref, ...), custom_call_target="tpu_custom_call", output_to_operand_aliasing={{0}: (2, {}), {1}: (3, {}), {2}: (4, {}), {3}: (5, {})} | custom-call | flops 1000000 | bytes 2097152 | tf_op jit(solution)/shard_map/finish_far/pallas_call | solution.py:612
  (3 shorter events, 0.1 us)
Async XLA Ops:
  3.3 7.9 %collective-permute-start = (bf16[224,384]{1,0:T(8,128)(2,1)}, bf16[224,384]{1,0:T(8,128)(2,1)S(1)}, u32[]{:S(2)}, u32[]{:S(2)}) collective-permute-start(bf16[224,384]{1,0:T(8,128)(2,1)} %get-tuple-element.41), channel_id=1, source_target_pairs={{0,1},{1,2},{2,3},{3,0},{4,5},{5,6},{6,7},{7,4},{8,9},{9,10},{10,1... | collective-permute-start | bytes 516104 | tf_op jit(solution)/shard_map/ppermute | solution.py:670
  3.8 9.2 %collective-permute-start.1 = (bf16[80,384]{1,0:T(8,128)(2,1)}, bf16[80,384]{1,0:T(8,128)(2,1)S(1)}, u32[]{:S(2)}, u32[]{:S(2)}) collective-permute-start(bf16[80,384]{1,0:T(8,128)(2,1)} %get-tuple-element.42), channel_id=1, source_target_pairs={{0,4},{1,5},{2,6},{3,7},{4,8},{5,9},{6,10},{7,11},{8,12},{9,13},{1... | collective-permute-start | bytes 184328 | tf_op jit(solution)/shard_map/ppermute | solution.py:670
  6.4 7.9 %collective-permute-start.2 = (bf16[80,384]{1,0:T(8,128)(2,1)}, bf16[80,384]{1,0:T(8,128)(2,1)S(1)}, u32[]{:S(2)}, u32[]{:S(2)}) collective-permute-start(bf16[80,384]{1,0:T(8,128)(2,1)} %get-tuple-element.43), channel_id=1, source_target_pairs={{0,5},{1,6},{2,7},{3,4},{4,9},{5,10},{6,11},{7,8},{8,13},{9,14},{1... | collective-permute-start | bytes 184328 | tf_op jit(solution)/shard_map/ppermute | solution.py:670
  8.8 1.0 %copy-start.4 = (f32[1,2,6,144,23]{3,1,4,2,0:T(2,128)S(1)}, f32[1,2,6,144,23]{3,1,4,2,0:T(2,128)}, u32[]{:S(2)}) copy-start(f32[1,2,6,144,23]{3,1,4,2,0:T(2,128)} %param.19) | copy-start | bytes 476932
  9.8 1.4 %copy-start.5 = (bf16[192,576]{1,0:T(8,128)(2,1)S(1)}, bf16[192,576]{1,0:T(8,128)(2,1)}, u32[]{:S(2)}) copy-start(bf16[192,576]{1,0:T(8,128)(2,1)} %refs_5_.1) | copy-start | bytes 663556
  9.8 1.4 %copy-start.6 = (bf16[192,192]{1,0:T(8,128)(2,1)S(1)}, bf16[192,192]{1,0:T(8,128)(2,1)}, u32[]{:S(2)}) copy-start(bf16[192,192]{1,0:T(8,128)(2,1)} %refs_6_.1) | copy-start | bytes 221188
  9.8 1.5 %copy-start.7 = (bf16[224,384]{1,0:T(8,128)(2,1)S(1)}, bf16[224,384]{1,0:T(8,128)(2,1)}, u32[]{:S(2)}) copy-start(bf16[224,384]{1,0:T(8,128)(2,1)} %get-tuple-element.40.own_ref.refs_0_) | copy-start | bytes 516100
  11.2 3.1 %copy-start.2 = (bf16[192,768]{1,0:T(8,128)(2,1)S(1)}, bf16[192,768]{1,0:T(8,128)(2,1)}, u32[]{:S(2)}) copy-start(bf16[192,768]{1,0:T(8,128)(2,1)} %refs_7_.1) | copy-start | bytes 884740
  11.2 3.1 %copy-start.3 = (bf16[768,192]{0,1:T(8,128)(2,1)S(1)}, bf16[768,192]{0,1:T(8,128)(2,1)}, u32[]{:S(2)}) copy-start(bf16[768,192]{0,1:T(8,128)(2,1)} %param.18) | copy-start | bytes 884740
  21.9 20.0 %copy-start.1 = (s32[1,576]{1,0:T(1,128)S(1)}, s32[1,576]{1,0:T(1,128)}, u32[]{:S(2)}) copy-start(s32[1,576]{1,0:T(1,128)} %constant.5.clone.perm_ref) | copy-start | bytes 6916
  21.9 3.8 %collective-permute-start.4 = (bf16[288,768]{1,0:T(8,128)(2,1)S(1)}, bf16[288,768]{1,0:T(8,128)(2,1)S(1)}, u32[]{:S(2)}, u32[]{:S(2)}) collective-permute-start(bf16[288,768]{1,0:T(8,128)(2,1)S(1)} %get-tuple-element.58), channel_id=1, source_target_pairs={{0,1},{1,0},{2,3},{3,2},{4,5},{5,4},{6,7},{7,6},{8,9},{9,8},{10,11... | collective-permute-start | bytes 1327112 | tf_op jit(solution)/shard_map/ppermute | solution.py:670
  22.1 3.6 %collective-permute-start.3 = (bf16[152,384]{1,0:T(8,128)(2,1)S(1)}, bf16[152,384]{1,0:T(8,128)(2,1)S(1)}, u32[]{:S(2)}, u32[]{:S(2)}) collective-permute-start(bf16[152,384]{1,0:T(8,128)(2,1)S(1)} %get-tuple-element.55), channel_id=1, source_target_pairs={{0,3},{1,0},{2,1},{3,2},{4,7},{5,4},{6,5},{7,6},{8,11},{9,8},{10,9... | collective-permute-start | bytes 350216 | tf_op jit(solution)/shard_map/ppermute | solution.py:670
  25.8 7.0 %collective-permute-start.5 = (bf16[72,768]{1,0:T(8,128)(2,1)S(1)}, bf16[72,768]{1,0:T(8,128)(2,1)S(1)}, u32[]{:S(2)}, u32[]{:S(2)}) collective-permute-start(bf16[72,768]{1,0:T(8,128)(2,1)S(1)} %get-tuple-element.60), channel_id=1, source_target_pairs={{0,6},{1,7},{2,4},{3,5},{4,2},{5,3},{6,0},{7,1},{8,14},{9,15},{10,... | collective-permute-start | bytes 331784 | tf_op jit(solution)/shard_map/ppermute | solution.py:670
  26.4 7.9 %collective-permute-start.6 = (bf16[72,768]{1,0:T(8,128)(2,1)S(1)}, bf16[72,768]{1,0:T(8,128)(2,1)S(1)}, u32[]{:S(2)}, u32[]{:S(2)}) collective-permute-start(bf16[72,768]{1,0:T(8,128)(2,1)S(1)} %get-tuple-element.61), channel_id=1, source_target_pairs={{0,2},{1,3},{2,0},{3,1},{4,6},{5,7},{6,4},{7,5},{8,10},{9,11},{10,... | collective-permute-start | bytes 331784 | tf_op jit(solution)/shard_map/ppermute | solution.py:670
  26.9 7.4 %collective-permute-start.7 = (bf16[72,768]{1,0:T(8,128)(2,1)S(1)}, bf16[72,768]{1,0:T(8,128)(2,1)S(1)}, u32[]{:S(2)}, u32[]{:S(2)}) collective-permute-start(bf16[72,768]{1,0:T(8,128)(2,1)S(1)} %get-tuple-element.62), channel_id=1, source_target_pairs={{0,4},{1,5},{2,6},{3,7},{4,0},{5,1},{6,2},{7,3},{8,12},{9,13},{10,... | collective-permute-start | bytes 331784 | tf_op jit(solution)/shard_map/ppermute | solution.py:670
  34.4 5.8 %collective-permute-start.9 = (bf16[440,128]{1,0:T(8,128)(2,1)S(1)}, bf16[440,128]{1,0:T(8,128)(2,1)S(1)}, u32[]{:S(2)}, u32[]{:S(2)}) collective-permute-start(bf16[440,128]{1,0:T(8,128)(2,1)S(1)} %chip_add.1.refs_0_.one_ref), channel_id=1, source_target_pairs={{0,8},{1,9},{2,10},{3,11},{4,12},{5,13},{6,14},{7,15},{8,0},{9,1},... | collective-permute-start | bytes 337928 | tf_op jit(solution)/shard_map/ppermute | solution.py:670
  35.0 5.1 %collective-permute-start.8 = (bf16[80,384]{1,0:T(8,128)(2,1)S(1)}, bf16[80,384]{1,0:T(8,128)(2,1)S(1)}, u32[]{:S(2)}, u32[]{:S(2)}) collective-permute-start(bf16[80,384]{1,0:T(8,128)(2,1)S(1)} %side.1), channel_id=1, source_target_pairs={{0,28},{1,29},{2,30},{3,31},{4,0},{5,1},{6,2},{7,3},{8,4},{9,5},{1... | collective-permute-start | bytes 184328 | tf_op jit(solution)/shard_map/ppermute | solution.py:670
  40.2 7.3 %collective-permute-start.10 = (bf16[440,128]{1,0:T(8,128)(2,1)S(1)}, bf16[440,128]{1,0:T(8,128)(2,1)S(1)}, u32[]{:S(2)}, u32[]{:S(2)}) collective-permute-start(bf16[440,128]{1,0:T(8,128)(2,1)S(1)} %deep_add.2.one_ref), channel_id=1, source_target_pairs={{0,16},{1,17},{2,18},{3,19},{4,20},{5,21},{6,22},{7,23},{8,24},{9,... | collective-permute-start | bytes 337928 | tf_op jit(solution)/shard_map/ppermute | solution.py:670
  47.5 1.0 %copy-start = (bf16[576,192]{1,0:T(8,128)(2,1)S(1)}, bf16[576,192]{1,0:T(8,128)(2,1)}, u32[]{:S(2)}) copy-start(bf16[576,192]{1,0:T(8,128)(2,1)} %to_home.1.refs_0_) | copy-start | bytes 663556
  48.5 6.2 %collective-permute-start.13 = (bf16[440,128]{1,0:T(8,128)(2,1)S(1)}, bf16[440,128]{1,0:T(8,128)(2,1)S(1)}, u32[]{:S(2)}, u32[]{:S(2)}) collective-permute-start(bf16[440,128]{1,0:T(8,128)(2,1)S(1)} %deep_add.3.refs_0_), channel_id=1, source_target_pairs={{0,6},{1,7},{2,4},{3,5},{4,2},{5,3},{6,0},{7,1},{8,14},{9,15},{10,... | collective-permute-start | bytes 337928 | tf_op jit(solution)/shard_map/ppermute | solution.py:670
  51.6 5.2 %collective-permute-start.12 = (bf16[440,128]{1,0:T(8,128)(2,1)S(1)}, bf16[440,128]{1,0:T(8,128)(2,1)S(1)}, u32[]{:S(2)}, u32[]{:S(2)}) collective-permute-start(bf16[440,128]{1,0:T(8,128)(2,1)S(1)} %deep_add.3.refs_0_), channel_id=1, source_target_pairs={{0,2},{1,3},{2,0},{3,1},{4,6},{5,7},{6,4},{7,5},{8,10},{9,11},{10,... | collective-permute-start | bytes 337928 | tf_op jit(solution)/shard_map/ppermute | solution.py:670
  52.3 4.8 %collective-permute-start.11 = (bf16[440,128]{1,0:T(8,128)(2,1)S(1)}, bf16[440,128]{1,0:T(8,128)(2,1)S(1)}, u32[]{:S(2)}, u32[]{:S(2)}) collective-permute-start(bf16[440,128]{1,0:T(8,128)(2,1)S(1)} %deep_add.3.refs_0_), channel_id=1, source_target_pairs={{0,4},{1,5},{2,6},{3,7},{4,0},{5,1},{6,2},{7,3},{8,12},{9,13},{10,... | collective-permute-start | bytes 337928 | tf_op jit(solution)/shard_map/ppermute | solution.py:670
  57.1 1.9 %collective-permute-start.14 = (bf16[1760,128]{1,0:T(8,128)(2,1)S(1)}, bf16[1760,128]{1,0:T(8,128)(2,1)S(1)}, u32[]{:S(2)}, u32[]{:S(2)}) collective-permute-start(bf16[1760,128]{1,0:T(8,128)(2,1)S(1)} %join.1.chunks_ref), channel_id=1, source_target_pairs={{0,1},{1,0},{2,3},{3,2},{4,5},{5,4},{6,7},{7,6},{8,9},{9,8},{10,11... | collective-permute-start | bytes 1351688 | tf_op jit(solution)/shard_map/ppermute | solution.py:670
where the time goes:
time: 60.2 us; the launch traced here: 60 us
  waiting for transfers between devices  20.4 us (34%)
  starting transfers between devices  19.8 us (33%)
  Pallas kernels  17 us (28%)
  local copies, waits for them, and re-layouts  1.95 us (3%)
  between operations  0.78 us (1%)
    ppermute x15, waiting for transfers between devices, send(): return lax.ppermute(value, AXES, pairs)  20.4 us
    ppermute x15, starting transfers between devices, send(): return lax.ppermute(value, AXES, pairs)  19.8 us
    pallas_call x1, Pallas kernels, block(): pl.pallas_call(functools.partial(block_kernel, lon_windows, sizes), out_s...  7.58 us
    pallas_call x1, Pallas kernels, pack(): pl.pallas_call(functools.partial(pack_kernel, rows, cols), out_shape=[sha...  2.67 us
    pallas_call x2, Pallas kernels, finish(): pl.pallas_call(functools.partial(finish_kernel, bool(before)), out_shape=...  2.08 us
    unnamed x16, local copies, waits for them, and re-layouts  1.95 us
    pallas_call x1, Pallas kernels, near_block(): pl.pallas_call(functools.partial(near_kernel, lon_windows), out_shape=[sh...  1.79 us
    pallas_call x1, Pallas kernels, expand_bias(): pl.pallas_call(functools.partial(bias_kernel, levels), out_shape=shape((g...  1.42 us
  transfers between devices with their start and end apart: 15, of which 11 were waited for; matrix products, arithmetic and copies ran while one was open for 0% of the time, Pallas kernels for 9%

commit v1 on v0

--- a/solution.py
+++ b/solution.py
@@ -503,7 +503,7 @@
     refs[-1][...] = jnp.concatenate([side_ref[...].astype(f32), corner], axis=0).astype(bf16)
 
 
-def home_kernel(sizes, own_ref, north_ref, side_ref, perm_ref, out_ref):
+def home_kernel(sizes, own_ref, north_ref, side_ref, perm_ref, out_ref, done_ref):
     wide = [ref[...].astype(f32) for ref in (own_ref, north_ref, side_ref)]
     half = wide[2].shape[0] // 2
     wide = [wide[0], wide[1][:-half], wide[2][:half], wide[2][half:]]
@@ -512,6 +512,7 @@
         pieces += [value[:, :C], value[: size - value.shape[0], C:]]
     pieces = jnp.concatenate(pieces, axis=0).astype(bf16)
     out_ref[...] = mm(one_hot(perm_ref), pieces).astype(bf16)
+    done_ref[...] = jnp.zeros_like(done_ref)
 
 
 def to_home(own, north, side, sizes, rows, cols):
@@ -519,9 +520,9 @@
     perm = spots(np.argsort(np.concatenate(piece_rows(rows, cols))))
     return pl.pallas_call(
         functools.partial(home_kernel, sizes),
-        out_shape=shape((count, C), bf16),
+        out_shape=[shape((count, C), bf16), shape((8, 128), f32)],
         in_specs=vmem(4),
-        out_specs=vmem(1)[0],
+        out_specs=vmem(2),
         compiler_params=pltpu.CompilerParams(vmem_limit_bytes=32 * MIB),
         cost_estimate=cost(2 * count * count * C, 4 * MIB),
         name="to_home",
@@ -646,8 +647,8 @@
     (total,) = small_call(chip_add_kernel, full, (own, *gots, land), "chip_add")
     (side,) = small_call(side_kernel, [shape((2 * side.shape[0], 2 * C), bf16)], (side, north), "side", after=(total,))
     side = shift(side, move=lambda lon, lat: (lon - 1, lat))
-    grad_tokens = go_home(north, side)
-    reach, waits = 1, [(side,), (grad_tokens,)]
+    grad_tokens, done = go_home(north, side)
+    reach, waits = 1, [(side,), (done,)]
     while reach < lon_count // 2:
         got = shift(total, move=deep_move(reach))
         reach *= 2

time: 60.2 us -> 59.2 us (0.983)
  local copies, waits for them, and re-layouts: 1.95 us -> 0.99 us
    unnamed x16 -> x14, local copies, waits for them, and re-layouts: 1.95 us -> 0.99 us
where the time goes in v1:
time: 59.2 us; the launch traced here: 59.1 us
  waiting for transfers between devices  20.5 us (35%)
  starting transfers between devices  19.8 us (33%)
  Pallas kernels  17 us (29%)
  local copies, waits for them, and re-layouts  0.99 us (2%)
  between operations  0.78 us (1%)
    ppermute x15, waiting for transfers between devices, send(): return lax.ppermute(value, AXES, pairs)  20.5 us
    ppermute x15, starting transfers between devices, send(): return lax.ppermute(value, AXES, pairs)  19.8 us
    pallas_call x1, Pallas kernels, block(): pl.pallas_call(functools.partial(block_kernel, lon_windows, sizes), out_s...  7.57 us
    pallas_call x1, Pallas kernels, pack(): pl.pallas_call(functools.partial(pack_kernel, rows, cols), out_shape=[sha...  2.67 us
    pallas_call x2, Pallas kernels, finish(): pl.pallas_call(functools.partial(finish_kernel, bool(before)), out_shape=...  2.08 us
    pallas_call x1, Pallas kernels, near_block(): pl.pallas_call(functools.partial(near_kernel, lon_windows), out_shape=[sh...  1.78 us
    pallas_call x1, Pallas kernels, expand_bias(): pl.pallas_call(functools.partial(bias_kernel, levels), out_shape=shape((g...  1.42 us
    pallas_call x1, Pallas kernels, to_home(): pl.pallas_call(functools.partial(home_kernel, sizes), out_shape=[shape((c...  1.19 us
  transfers between devices with their start and end apart: 15, of which 11 were waited for; matrix products, arithmetic and copies ran while one was open for 0% of the time, Pallas kernels for 9%

profile of v1, /device:TPU:0, one launch (start us, length us, event | category | flops | bytes accessed | tf_op | source)
XLA Modules:
  0.0 59.1 jit_solution(14377297985988790988)
XLA Ops:
  0.6 2.7 %pack.1 = (bf16[224,384]{1,0:T(8,128)(2,1)}, bf16[224,384]{1,0:T(8,128)(2,1)}, bf16[80,384]{1,0:T(8,128)(2,1)}, bf16[80,384]{1,0:T(8,128)(2,1)}) custom-call(bf16[576,192]{1,0:T(8,128)(2,1)} %bitcast.15, bf16[576,192]{1,0:T(8,128)(2,1)} %bitcast.16, s32[6,24]{1,0:T(8,128)} %refs_2_.2, f32[1,192]{1,0:T(1,128)} %bitcast.17, s32[1,576]{1,0:T(1,128)} %constant.4.clone.refs_4_), custom_call_target="tpu_custom_call" | custom-call | flops 254803968 | bytes 4194304 | tf_op jit(solution)/shard_map/pack/pallas_call | solution.py:170
  3.3 0.5 collective-permute-start
  3.8 2.6 %collective-permute-start.1 = (bf16[80,384]{1,0:T(8,128)(2,1)}, bf16[80,384]{1,0:T(8,128)(2,1)S(1)}, u32[]{:S(2)}, u32[]{:S(2)}) collective-permute-start(bf16[80,384]{1,0:T(8,128)(2,1)} %get-tuple-element.44), channel_id=1, source_target_pairs={{0,4},{1,5},{2,6},{3,7},{4,8},{5,9},{6,10},{7,11},{8,12},{9,13},{1... | collective-permute-start | bytes 184328 | tf_op jit(solution)/shard_map/ppermute | solution.py:671
  6.4 2.4 %collective-permute-start.2 = (bf16[80,384]{1,0:T(8,128)(2,1)}, bf16[80,384]{1,0:T(8,128)(2,1)S(1)}, u32[]{:S(2)}, u32[]{:S(2)}) collective-permute-start(bf16[80,384]{1,0:T(8,128)(2,1)} %get-tuple-element.45), channel_id=1, source_target_pairs={{0,5},{1,6},{2,7},{3,4},{4,9},{5,10},{6,11},{7,8},{8,13},{9,14},{1... | collective-permute-start | bytes 184328 | tf_op jit(solution)/shard_map/ppermute | solution.py:671
  8.8 0.0 copy-start.2
  8.8 1.0 %copy-done.2 = f32[1,2,6,144,23]{3,1,4,2,0:T(2,128)S(1)} copy-done((f32[1,2,6,144,23]{3,1,4,2,0:T(2,128)S(1)}, f32[1,2,6,144,23]{3,1,4,2,0:T(2,128)}, u32[]{:S(2)}) %copy-start.2) | copy-done | bytes 159000
  9.8 0.0 copy-start.3
  9.8 0.0 copy-start.4
  9.8 0.0 copy-start.6
  9.8 1.4 %bias.1.refs_0_.refs_4_ = f32[12,144,144]{2,1,0:T(8,128)S(1)} custom-call(f32[138,2,144]{2,1,0:T(2,128)S(1)} %bitcast.13), custom_call_target="tpu_custom_call" | custom-call | flops 1000000000 | bytes 8388608 | tf_op jit(solution)/shard_map/bias/pallas_call | solution.py:259
  11.2 0.0 collective-permute-done.north_ref.refs_1_
  11.2 0.0 copy-done.3
  11.2 0.0 copy-done.4
  11.2 0.0 copy-done.6
  11.2 0.0 copy-start
  11.2 0.0 copy-start.1
  11.3 1.8 %near_block.1 = (bf16[288,192]{1,0:T(8,128)(2,1)S(1)}, bf16[288,192]{1,0:T(8,128)(2,1)S(1)}, bf16[288,192]{1,0:T(8,128)(2,1)S(1)}, bf16[12,144,144]{2,1,0:T(8,12...) custom-call(bf16[224,384]{1,0:T(8,128)(2,1)S(1)} %copy-done.6, ...), custom_call_target="tpu_custom_call" | custom-call | flops 3000000000 | bytes 8388608 | tf_op jit(solution)/shard_map/near_block/pallas_call | solution.py:446
  13.0 0.0 collective-permute-done.1.refs_2_
  13.1 1.2 %collective-permute-done.2.refs_3_ = bf16[80,384]{1,0:T(8,128)(2,1)S(1)} collective-permute-done((bf16[80,384]{1,0:T(8,128)(2,1)}, bf16[80,384]{1,0:T(8,128)(2,1)S(1)}, u32[]{:S(2)}, u32[]{:S(2)}) %collective-permute-start.2) | collective-permute-done | bytes 61472 | tf_op jit(solution)/shard_map/ppermute | solution.py:671
  14.3 0.0 copy-done
  14.3 0.0 copy-done.1
  14.3 7.6 %block.1 = (bf16[112,384]{1,0:T(8,128)(2,1)S(1)}, bf16[152,384]{1,0:T(8,128)(2,1)S(1)}, bf16[40,384]{1,0:T(8,128)(2,1)S(1)}, f32[1,192]{1,0:T(1,128)S(1)}, f32[2...) custom-call(bf16[224,384]{1,0:T(8,128)(2,1)S(1)} %copy-done.6, ...), custom_call_target="tpu_custom_call" | custom-call | flops 8000000000 | bytes 16777216 | tf_op jit(solution)/shard_map/block/pallas_call | solution.py:485
  21.9 0.0 copy-start.5
  21.9 0.2 collective-permute-start.4
  22.1 1.3 %collective-permute-start.3 = (bf16[152,384]{1,0:T(8,128)(2,1)S(1)}, bf16[152,384]{1,0:T(8,128)(2,1)S(1)}, u32[]{:S(2)}, u32[]{:S(2)}) collective-permute-start(bf16[152,384]{1,0:T(8,128)(2,1)S(1)} %get-tuple-element.57), channel_id=1, source_target_pairs={{0,3},{1,0},{2,1},{3,2},{4,7},{5,4},{6,5},{7,6},{8,11},{9,8},{10,9... | collective-permute-start | bytes 350216 | tf_op jit(solution)/shard_map/ppermute | solution.py:671
  23.3 2.4 %collective-permute-done.3.refs_0_.north_ref = bf16[152,384]{1,0:T(8,128)(2,1)S(1)} collective-permute-done((bf16[152,384]{1,0:T(8,128)(2,1)S(1)}, bf16[152,384]{1,0:T(8,128)(2,1)S(1)}, u32[]{:S(2)}, u32[]{:S(2)}) %collective-permute-start.3) | collective-permute-done | bytes 116768 | tf_op jit(solution)/shard_map/ppermute | solution.py:671
  25.7 0.0 collective-permute-done.4.got_ref
  25.7 0.1 core_add.1
  25.8 0.6 collective-permute-start.5
  26.4 0.5 collective-permute-start.6
  26.9 2.5 %collective-permute-start.7 = (bf16[72,768]{1,0:T(8,128)(2,1)S(1)}, bf16[72,768]{1,0:T(8,128)(2,1)S(1)}, u32[]{:S(2)}, u32[]{:S(2)}) collective-permute-start(bf16[72,768]{1,0:T(8,128)(2,1)S(1)} %get-tuple-element.64), channel_id=1, source_target_pairs={{0,4},{1,5},{2,6},{3,7},{4,0},{5,1},{6,2},{7,3},{8,12},{9,13},{10,... | collective-permute-start | bytes 331784 | tf_op jit(solution)/shard_map/ppermute | solution.py:671
  29.4 3.4 %collective-permute-done.5.refs_0_ = bf16[72,768]{1,0:T(8,128)(2,1)S(1)} collective-permute-done((bf16[72,768]{1,0:T(8,128)(2,1)S(1)}, bf16[72,768]{1,0:T(8,128)(2,1)S(1)}, u32[]{:S(2)}, u32[]{:S(2)}) %collective-permute-start.5) | collective-permute-done | bytes 110624 | tf_op jit(solution)/shard_map/ppermute | solution.py:671
  32.8 1.5 %collective-permute-done.6.refs_1_ = bf16[72,768]{1,0:T(8,128)(2,1)S(1)} collective-permute-done((bf16[72,768]{1,0:T(8,128)(2,1)S(1)}, bf16[72,768]{1,0:T(8,128)(2,1)S(1)}, u32[]{:S(2)}, u32[]{:S(2)}) %collective-permute-start.6) | collective-permute-done | bytes 110624 | tf_op jit(solution)/shard_map/ppermute | solution.py:671
  34.3 0.0 collective-permute-done.7.refs_2_
  34.3 0.1 chip_add.1.refs_0_.one_ref
  34.4 0.6 %collective-permute-start.9 = (bf16[440,128]{1,0:T(8,128)(2,1)S(1)}, bf16[440,128]{1,0:T(8,128)(2,1)S(1)}, u32[]{:S(2)}, u32[]{:S(2)}) collective-permute-start(bf16[440,128]{1,0:T(8,128)(2,1)S(1)} %chip_add.1.refs_0_.one_ref), channel_id=1, source_target_pairs={{0,8},{1,9},{2,10},{3,11},{4,12},{5,13},{6,14},{7,15},{8,0},{9,1},... | collective-permute-start | bytes 337928 | tf_op jit(solution)/shard_map/ppermute | solution.py:671
  35.0 3.2 %collective-permute-start.8 = (bf16[80,384]{1,0:T(8,128)(2,1)S(1)}, bf16[80,384]{1,0:T(8,128)(2,1)S(1)}, u32[]{:S(2)}, u32[]{:S(2)}) collective-permute-start(bf16[80,384]{1,0:T(8,128)(2,1)S(1)} %side.1), channel_id=1, source_target_pairs={{0,28},{1,29},{2,30},{3,31},{4,0},{5,1},{6,2},{7,3},{8,4},{9,5},{1... | collective-permute-start | bytes 184328 | tf_op jit(solution)/shard_map/ppermute | solution.py:671
  38.3 1.9 %collective-permute-done.8.side_ref.refs_0_ = bf16[80,384]{1,0:T(8,128)(2,1)S(1)} collective-permute-done((bf16[80,384]{1,0:T(8,128)(2,1)S(1)}, bf16[80,384]{1,0:T(8,128)(2,1)S(1)}, u32[]{:S(2)}, u32[]{:S(2)}) %collective-permute-start.8) | collective-permute-done | bytes 61472 | tf_op jit(solution)/shard_map/ppermute | solution.py:671
  40.1 0.1 collective-permute-done.9.two_ref
  40.2 1.6 %collective-permute-start.10 = (bf16[440,128]{1,0:T(8,128)(2,1)S(1)}, bf16[440,128]{1,0:T(8,128)(2,1)S(1)}, u32[]{:S(2)}, u32[]{:S(2)}) collective-permute-start(bf16[440,128]{1,0:T(8,128)(2,1)S(1)} %deep_add.2.one_ref), channel_id=1, source_target_pairs={{0,16},{1,17},{2,18},{3,19},{4,20},{5,21},{6,22},{7,23},{8,24},{9,... | collective-permute-start | bytes 337928 | tf_op jit(solution)/shard_map/ppermute | solution.py:671
  41.8 0.0 copy-done.5
  41.9 1.2 %to_home.1 = (bf16[576,192]{1,0:T(8,128)(2,1)}, f32[8,128]{1,0:T(8,128)S(1)}) custom-call(bf16[112,384]{1,0:T(8,128)(2,1)S(1)} %get-tuple-element.56.own_ref, bf16[152,384]{1,0:T(8,128)(2,1)S(1)} %collective-permute-done.3.refs_0_.north_ref, bf16[80,384]{1,0:T(8,128)(2,1)S(1)} %collective-permute-done.8.side_ref.refs_0_, s32[1,576]{1,0:T(1,128)S(1)} %copy-done.5), custom_call_target="tpu_custom_call" | custom-call | flops 127401984 | bytes 4194304 | tf_op jit(solution)/shard_map/to_home/pallas_call | solution.py:521
  43.0 4.5 %collective-permute-done.10.two_ref = bf16[440,128]{1,0:T(8,128)(2,1)S(1)} collective-permute-done((bf16[440,128]{1,0:T(8,128)(2,1)S(1)}, bf16[440,128]{1,0:T(8,128)(2,1)S(1)}, u32[]{:S(2)}, u32[]{:S(2)}) %collective-permute-start.10) | collective-permute-done | bytes 112672 | tf_op jit(solution)/shard_map/ppermute | solution.py:671
  47.5 3.1 %collective-permute-start.13 = (bf16[440,128]{1,0:T(8,128)(2,1)S(1)}, bf16[440,128]{1,0:T(8,128)(2,1)S(1)}, u32[]{:S(2)}, u32[]{:S(2)}) collective-permute-start(bf16[440,128]{1,0:T(8,128)(2,1)S(1)} %deep_add.3.refs_0_), channel_id=1, source_target_pairs={{0,6},{1,7},{2,4},{3,5},{4,2},{5,3},{6,0},{7,1},{8,14},{9,15},{10,... | collective-permute-start | bytes 337928 | tf_op jit(solution)/shard_map/ppermute | solution.py:671
  50.6 0.6 %collective-permute-start.12 = (bf16[440,128]{1,0:T(8,128)(2,1)S(1)}, bf16[440,128]{1,0:T(8,128)(2,1)S(1)}, u32[]{:S(2)}, u32[]{:S(2)}) collective-permute-start(bf16[440,128]{1,0:T(8,128)(2,1)S(1)} %deep_add.3.refs_0_), channel_id=1, source_target_pairs={{0,2},{1,3},{2,0},{3,1},{4,6},{5,7},{6,4},{7,5},{8,10},{9,11},{10,... | collective-permute-start | bytes 337928 | tf_op jit(solution)/shard_map/ppermute | solution.py:671
  51.3 0.0 collective-permute-start.11
  51.3 2.4 %collective-permute-done.13.refs_3_ = bf16[440,128]{1,0:T(8,128)(2,1)S(1)} collective-permute-done((bf16[440,128]{1,0:T(8,128)(2,1)S(1)}, bf16[440,128]{1,0:T(8,128)(2,1)S(1)}, u32[]{:S(2)}, u32[]{:S(2)}) %collective-permute-start.13) | collective-permute-done | bytes 112672 | tf_op jit(solution)/shard_map/ppermute | solution.py:671
  53.7 2.1 %collective-permute-done.12.refs_2_ = bf16[440,128]{1,0:T(8,128)(2,1)S(1)} collective-permute-done((bf16[440,128]{1,0:T(8,128)(2,1)S(1)}, bf16[440,128]{1,0:T(8,128)(2,1)S(1)}, u32[]{:S(2)}, u32[]{:S(2)}) %collective-permute-start.12) | collective-permute-done | bytes 112672 | tf_op jit(solution)/shard_map/ppermute | solution.py:671
  55.8 0.3 collective-permute-done.11.refs_1_
  56.1 0.1 join.1.chunks_ref
  56.1 0.1 collective-permute-start.14
  56.2 1.0 %finish_own.1 = (f32[192,576]{1,0:T(8,128)}, f32[192,192]{1,0:T(8,128)}, f32[192,768]{1,0:T(8,128)}, f32[192,768]{1,0:T(8,128)}, f32[1,192]{1,0:T(1,128)S(1)}) custom-call(bf16[1760,128]{1,0:T(8,128)(2,1)S(1)} %join.1.chunks_ref), custom_call_target="tpu_custom_call" | custom-call | flops 1000000 | bytes 2097152 | tf_op jit(solution)/shard_map/finish_own/pallas_call | solution.py:613
  57.3 0.7 %collective-permute-done.14.chunks_ref = bf16[1760,128]{1,0:T(8,128)(2,1)S(1)} collective-permute-done((bf16[1760,128]{1,0:T(8,128)(2,1)S(1)}, bf16[1760,128]{1,0:T(8,128)(2,1)S(1)}, u32[]{:S(2)}, u32[]{:S(2)}) %collective-permute-start.14) | collective-permute-done | bytes 450592 | tf_op jit(solution)/shard_map/ppermute | solution.py:671
  58.0 1.0 %finish_far.1 = (f32[192,576]{1,0:T(8,128)}, f32[192,192]{1,0:T(8,128)}, f32[192,768]{1,0:T(8,128)}, f32[192,768]{1,0:T(8,128)}, f32[1,192]{1,0:T(1,128)}) custom-call(bf16[1760,128]{1,0:T(8,128)(2,1)S(1)} %collective-permute-done.14.chunks_ref, ...), custom_call_target="tpu_custom_call", output_to_operand_aliasing={{0}: (2, {}), {1}: (3, {}), {2}: (4, {}), {3}: (5, {})} | custom-call | flops 1000000 | bytes 2097152 | tf_op jit(solution)/shard_map/finish_far/pallas_call | solution.py:613
  (3 shorter events, 0.1 us)
Async XLA Ops:
  3.3 7.9 %collective-permute-start = (bf16[224,384]{1,0:T(8,128)(2,1)}, bf16[224,384]{1,0:T(8,128)(2,1)S(1)}, u32[]{:S(2)}, u32[]{:S(2)}) collective-permute-start(bf16[224,384]{1,0:T(8,128)(2,1)} %get-tuple-element.43), channel_id=1, source_target_pairs={{0,1},{1,2},{2,3},{3,0},{4,5},{5,6},{6,7},{7,4},{8,9},{9,10},{10,1... | collective-permute-start | bytes 516104 | tf_op jit(solution)/shard_map/ppermute | solution.py:671
  3.8 9.2 %collective-permute-start.1 = (bf16[80,384]{1,0:T(8,128)(2,1)}, bf16[80,384]{1,0:T(8,128)(2,1)S(1)}, u32[]{:S(2)}, u32[]{:S(2)}) collective-permute-start(bf16[80,384]{1,0:T(8,128)(2,1)} %get-tuple-element.44), channel_id=1, source_target_pairs={{0,4},{1,5},{2,6},{3,7},{4,8},{5,9},{6,10},{7,11},{8,12},{9,13},{1... | collective-permute-start | bytes 184328 | tf_op jit(solution)/shard_map/ppermute | solution.py:671
  6.4 7.9 %collective-permute-start.2 = (bf16[80,384]{1,0:T(8,128)(2,1)}, bf16[80,384]{1,0:T(8,128)(2,1)S(1)}, u32[]{:S(2)}, u32[]{:S(2)}) collective-permute-start(bf16[80,384]{1,0:T(8,128)(2,1)} %get-tuple-element.45), channel_id=1, source_target_pairs={{0,5},{1,6},{2,7},{3,4},{4,9},{5,10},{6,11},{7,8},{8,13},{9,14},{1... | collective-permute-start | bytes 184328 | tf_op jit(solution)/shard_map/ppermute | solution.py:671
  8.8 1.0 %copy-start.2 = (f32[1,2,6,144,23]{3,1,4,2,0:T(2,128)S(1)}, f32[1,2,6,144,23]{3,1,4,2,0:T(2,128)}, u32[]{:S(2)}) copy-start(f32[1,2,6,144,23]{3,1,4,2,0:T(2,128)} %param.19) | copy-start | bytes 476932
  9.8 1.4 %copy-start.3 = (bf16[192,576]{1,0:T(8,128)(2,1)S(1)}, bf16[192,576]{1,0:T(8,128)(2,1)}, u32[]{:S(2)}) copy-start(bf16[192,576]{1,0:T(8,128)(2,1)} %refs_5_.1) | copy-start | bytes 663556
  9.8 1.4 %copy-start.4 = (bf16[192,192]{1,0:T(8,128)(2,1)S(1)}, bf16[192,192]{1,0:T(8,128)(2,1)}, u32[]{:S(2)}) copy-start(bf16[192,192]{1,0:T(8,128)(2,1)} %refs_6_.1) | copy-start | bytes 221188
  9.8 1.5 %copy-start.6 = (bf16[224,384]{1,0:T(8,128)(2,1)S(1)}, bf16[224,384]{1,0:T(8,128)(2,1)}, u32[]{:S(2)}) copy-start(bf16[224,384]{1,0:T(8,128)(2,1)} %get-tuple-element.42.own_ref.refs_0_) | copy-start | bytes 516100
  11.2 3.1 %copy-start = (bf16[192,768]{1,0:T(8,128)(2,1)S(1)}, bf16[192,768]{1,0:T(8,128)(2,1)}, u32[]{:S(2)}) copy-start(bf16[192,768]{1,0:T(8,128)(2,1)} %refs_7_.1) | copy-start | bytes 884740
  11.2 3.1 %copy-start.1 = (bf16[768,192]{0,1:T(8,128)(2,1)S(1)}, bf16[768,192]{0,1:T(8,128)(2,1)}, u32[]{:S(2)}) copy-start(bf16[768,192]{0,1:T(8,128)(2,1)} %param.18) | copy-start | bytes 884740
  21.9 20.0 %copy-start.5 = (s32[1,576]{1,0:T(1,128)S(1)}, s32[1,576]{1,0:T(1,128)}, u32[]{:S(2)}) copy-start(s32[1,576]{1,0:T(1,128)} %constant.5.clone.perm_ref) | copy-start | bytes 6916
  21.9 3.8 %collective-permute-start.4 = (bf16[288,768]{1,0:T(8,128)(2,1)S(1)}, bf16[288,768]{1,0:T(8,128)(2,1)S(1)}, u32[]{:S(2)}, u32[]{:S(2)}) collective-permute-start(bf16[288,768]{1,0:T(8,128)(2,1)S(1)} %get-tuple-element.60), channel_id=1, source_target_pairs={{0,1},{1,0},{2,3},{3,2},{4,5},{5,4},{6,7},{7,6},{8,9},{9,8},{10,11... | collective-permute-start | bytes 1327112 | tf_op jit(solution)/shard_map/ppermute | solution.py:671
  22.1 3.6 %collective-permute-start.3 = (bf16[152,384]{1,0:T(8,128)(2,1)S(1)}, bf16[152,384]{1,0:T(8,128)(2,1)S(1)}, u32[]{:S(2)}, u32[]{:S(2)}) collective-permute-start(bf16[152,384]{1,0:T(8,128)(2,1)S(1)} %get-tuple-element.57), channel_id=1, source_target_pairs={{0,3},{1,0},{2,1},{3,2},{4,7},{5,4},{6,5},{7,6},{8,11},{9,8},{10,9... | collective-permute-start | bytes 350216 | tf_op jit(solution)/shard_map/ppermute | solution.py:671
  25.8 7.0 %collective-permute-start.5 = (bf16[72,768]{1,0:T(8,128)(2,1)S(1)}, bf16[72,768]{1,0:T(8,128)(2,1)S(1)}, u32[]{:S(2)}, u32[]{:S(2)}) collective-permute-start(bf16[72,768]{1,0:T(8,128)(2,1)S(1)} %get-tuple-element.62), channel_id=1, source_target_pairs={{0,6},{1,7},{2,4},{3,5},{4,2},{5,3},{6,0},{7,1},{8,14},{9,15},{10,... | collective-permute-start | bytes 331784 | tf_op jit(solution)/shard_map/ppermute | solution.py:671
  26.4 7.9 %collective-permute-start.6 = (bf16[72,768]{1,0:T(8,128)(2,1)S(1)}, bf16[72,768]{1,0:T(8,128)(2,1)S(1)}, u32[]{:S(2)}, u32[]{:S(2)}) collective-permute-start(bf16[72,768]{1,0:T(8,128)(2,1)S(1)} %get-tuple-element.63), channel_id=1, source_target_pairs={{0,2},{1,3},{2,0},{3,1},{4,6},{5,7},{6,4},{7,5},{8,10},{9,11},{10,... | collective-permute-start | bytes 331784 | tf_op jit(solution)/shard_map/ppermute | solution.py:671
  26.9 7.4 %collective-permute-start.7 = (bf16[72,768]{1,0:T(8,128)(2,1)S(1)}, bf16[72,768]{1,0:T(8,128)(2,1)S(1)}, u32[]{:S(2)}, u32[]{:S(2)}) collective-permute-start(bf16[72,768]{1,0:T(8,128)(2,1)S(1)} %get-tuple-element.64), channel_id=1, source_target_pairs={{0,4},{1,5},{2,6},{3,7},{4,0},{5,1},{6,2},{7,3},{8,12},{9,13},{10,... | collective-permute-start | bytes 331784 | tf_op jit(solution)/shard_map/ppermute | solution.py:671
  34.4 5.8 %collective-permute-start.9 = (bf16[440,128]{1,0:T(8,128)(2,1)S(1)}, bf16[440,128]{1,0:T(8,128)(2,1)S(1)}, u32[]{:S(2)}, u32[]{:S(2)}) collective-permute-start(bf16[440,128]{1,0:T(8,128)(2,1)S(1)} %chip_add.1.refs_0_.one_ref), channel_id=1, source_target_pairs={{0,8},{1,9},{2,10},{3,11},{4,12},{5,13},{6,14},{7,15},{8,0},{9,1},... | collective-permute-start | bytes 337928 | tf_op jit(solution)/shard_map/ppermute | solution.py:671
  35.0 5.1 %collective-permute-start.8 = (bf16[80,384]{1,0:T(8,128)(2,1)S(1)}, bf16[80,384]{1,0:T(8,128)(2,1)S(1)}, u32[]{:S(2)}, u32[]{:S(2)}) collective-permute-start(bf16[80,384]{1,0:T(8,128)(2,1)S(1)} %side.1), channel_id=1, source_target_pairs={{0,28},{1,29},{2,30},{3,31},{4,0},{5,1},{6,2},{7,3},{8,4},{9,5},{1... | collective-permute-start | bytes 184328 | tf_op jit(solution)/shard_map/ppermute | solution.py:671
  40.2 7.3 %collective-permute-start.10 = (bf16[440,128]{1,0:T(8,128)(2,1)S(1)}, bf16[440,128]{1,0:T(8,128)(2,1)S(1)}, u32[]{:S(2)}, u32[]{:S(2)}) collective-permute-start(bf16[440,128]{1,0:T(8,128)(2,1)S(1)} %deep_add.2.one_ref), channel_id=1, source_target_pairs={{0,16},{1,17},{2,18},{3,19},{4,20},{5,21},{6,22},{7,23},{8,24},{9,... | collective-permute-start | bytes 337928 | tf_op jit(solution)/shard_map/ppermute | solution.py:671
  47.5 6.2 %collective-permute-start.13 = (bf16[440,128]{1,0:T(8,128)(2,1)S(1)}, bf16[440,128]{1,0:T(8,128)(2,1)S(1)}, u32[]{:S(2)}, u32[]{:S(2)}) collective-permute-start(bf16[440,128]{1,0:T(8,128)(2,1)S(1)} %deep_add.3.refs_0_), channel_id=1, source_target_pairs={{0,6},{1,7},{2,4},{3,5},{4,2},{5,3},{6,0},{7,1},{8,14},{9,15},{10,... | collective-permute-start | bytes 337928 | tf_op jit(solution)/shard_map/ppermute | solution.py:671
  50.6 5.2 %collective-permute-start.12 = (bf16[440,128]{1,0:T(8,128)(2,1)S(1)}, bf16[440,128]{1,0:T(8,128)(2,1)S(1)}, u32[]{:S(2)}, u32[]{:S(2)}) collective-permute-start(bf16[440,128]{1,0:T(8,128)(2,1)S(1)} %deep_add.3.refs_0_), channel_id=1, source_target_pairs={{0,2},{1,3},{2,0},{3,1},{4,6},{5,7},{6,4},{7,5},{8,10},{9,11},{10,... | collective-permute-start | bytes 337928 | tf_op jit(solution)/shard_map/ppermute | solution.py:671
  51.3 4.8 %collective-permute-start.11 = (bf16[440,128]{1,0:T(8,128)(2,1)S(1)}, bf16[440,128]{1,0:T(8,128)(2,1)S(1)}, u32[]{:S(2)}, u32[]{:S(2)}) collective-permute-start(bf16[440,128]{1,0:T(8,128)(2,1)S(1)} %deep_add.3.refs_0_), channel_id=1, source_target_pairs={{0,4},{1,5},{2,6},{3,7},{4,0},{5,1},{6,2},{7,3},{8,12},{9,13},{10,... | collective-permute-start | bytes 337928 | tf_op jit(solution)/shard_map/ppermute | solution.py:671
  56.1 1.9 %collective-permute-start.14 = (bf16[1760,128]{1,0:T(8,128)(2,1)S(1)}, bf16[1760,128]{1,0:T(8,128)(2,1)S(1)}, u32[]{:S(2)}, u32[]{:S(2)}) collective-permute-start(bf16[1760,128]{1,0:T(8,128)(2,1)S(1)} %join.1.chunks_ref), channel_id=1, source_target_pairs={{0,1},{1,0},{2,3},{3,2},{4,5},{5,4},{6,7},{7,6},{8,9},{9,8},{10,11... | collective-permute-start | bytes 1351688 | tf_op jit(solution)/shard_map/ppermute | solution.py:671

commit v2 on v1

--- a/solution.py
+++ b/solution.py
@@ -180,9 +180,13 @@
             pltpu.VMEM((1, count), jnp.int32),
             pltpu.SemaphoreType.DMA((5,)),
         ],
+        compiler_params=pltpu.CompilerParams(vmem_limit_bytes=24 * MIB),
         cost_estimate=cost(4 * count * count * C, 4 * MIB),
         name="pack",
-    )(tokens.reshape(count, C), cotangent.reshape(count, C), land_sea, vector.reshape(1, C), perm)
+    )(*[
+        pltpu.with_memory_space_constraint(value, pltpu.HBM)
+        for value in (tokens.reshape(count, C), cotangent.reshape(count, C), land_sea, vector.reshape(1, C), perm)
+    ])
 
 
 def floor_div(values, divisor):
@@ -200,7 +204,9 @@
     return level * WH + half * HH + (spot - level * HH)
 
 
-def bias_kernel(levels, table_ref, out_ref, *wide_refs):
+def bias_kernel(levels, source_ref, out_ref, table_ref, sem, *wide_refs):
+    copy = pltpu.make_async_copy(source_ref, table_ref, sem)
+    copy.start()
     groups = levels * HEADS
     pairs = PLACES * PLACES
     row = lax.broadcasted_iota(jnp.int32, (HEADS * RELW, HEADS * STRIP), 0)
@@ -211,6 +217,7 @@
     row = lax.broadcasted_iota(jnp.int32, (pairs, pairs), 0)
     source = place_order(floor_div(row, PLACES)) * PLACES + remainder(row, PLACES)
     reorder = (lax.broadcasted_iota(jnp.int32, (pairs, pairs), 1) == source).astype(f32).astype(bf16)
+    copy.wait()
     for level in range(levels):
         table = table_ref[:, level, :].T
         high = table.astype(bf16)
@@ -259,13 +266,14 @@
     return pl.pallas_call(
         functools.partial(bias_kernel, levels),
         out_shape=shape((groups, TOK, TOK), f32),
-        in_specs=vmem(1),
+        in_specs=[pl.BlockSpec(memory_space=pltpu.HBM)],
         out_specs=vmem(1)[0],
-        scratch_shapes=[pltpu.VMEM((groups * pairs, 128), f32)] * (STRIP // 128),
+        scratch_shapes=[pltpu.VMEM(flat.shape, f32), pltpu.SemaphoreType.DMA]
+        + [pltpu.VMEM((groups * pairs, 128), f32)] * (STRIP // 128),
         compiler_params=pltpu.CompilerParams(vmem_limit_bytes=28 * MIB),
         cost_estimate=cost(10**9, 8 * MIB),
         name="bias",
-    )(flat)
+    )(pltpu.with_memory_space_constraint(flat, pltpu.HBM))
 
 
 def head_masks(count):

time: 59.2 us -> 58.4 us (0.986)
  local copies, waits for them, and re-layouts: 0.99 us -> 0.03 us
    pallas_call x1, Pallas kernels: 1.42 us -> 2.38 us  [expand_bias(): pl.pallas_call(functools.partial(bias_kernel, levels), out_shape=shape((g...]
    unnamed x14 -> x10, local copies, waits for them, and re-layouts: 0.99 us -> 0.03 us
    pallas_call x1, Pallas kernels: 2.67 us -> 2 us  [pack(): pl.pallas_call(functools.partial(pack_kernel, rows, cols), out_shape=[sha...]
  transfers between devices with their start and end apart: 15 -> 15, of which waited for: 11 -> 10; matrix products, arithmetic and copies ran while one was open for 0% -> 0% of each run, Pallas kernels for 9% -> 11%
where the time goes in v2:
time: 58.4 us; the launch traced here: 58.3 us
  waiting for transfers between devices  20.3 us (35%)
  starting transfers between devices  19.8 us (34%)
  Pallas kernels  17.3 us (30%)
  between operations  0.77 us (1%)
    ppermute x15, waiting for transfers between devices, send(): return lax.ppermute(value, AXES, pairs)  20.3 us
    ppermute x15, starting transfers between devices, send(): return lax.ppermute(value, AXES, pairs)  19.8 us
    pallas_call x1, Pallas kernels, block(): pl.pallas_call(functools.partial(block_kernel, lon_windows, sizes), out_s...  7.58 us
    pallas_call x1, Pallas kernels, expand_bias(): pl.pallas_call(functools.partial(bias_kernel, levels), out_shape=shape((g...  2.38 us
    pallas_call x2, Pallas kernels, finish(): pl.pallas_call(functools.partial(finish_kernel, bool(before)), out_shape=...  2.08 us
    pallas_call x1, Pallas kernels, pack(): pl.pallas_call(functools.partial(pack_kernel, rows, cols), out_shape=[sha...  2 us
    pallas_call x1, Pallas kernels, near_block(): pl.pallas_call(functools.partial(near_kernel, lon_windows), out_shape=[sh...  1.77 us
    pallas_call x1, Pallas kernels, to_home(): pl.pallas_call(functools.partial(home_kernel, sizes), out_shape=[shape((c...  1.19 us
  transfers between devices with their start and end apart: 15, of which 10 were waited for; matrix products, arithmetic and copies ran while one was open for 0% of the time, Pallas kernels for 11%

profile of v2, /device:TPU:0, one launch (start us, length us, event | category | flops | bytes accessed | tf_op | source)
XLA Modules:
  0.0 58.3 jit_solution(2232706343284064658)
XLA Ops:
  0.6 2.0 %pack.1 = (bf16[224,384]{1,0:T(8,128)(2,1)S(1)}, bf16[224,384]{1,0:T(8,128)(2,1)S(1)}, bf16[80,384]{1,0:T(8,128)(2,1)S(1)}, bf16[80,384]{1,0:T(8,128)(2,1)S(1)}) custom-call(bf16[576,192]{1,0:T(8,128)(2,1)} %bitcast.14, bf16[576,192]{1,0:T(8,128)(2,1)} %bitcast.15, s32[6,24]{1,0:T(8,128)} %refs_2_.2, f32[1,192]{1,0:T(1,128)} %bitcast.17, ...), custom_call_target="tpu_custom_call" | custom-call | flops 254803968 | bytes 4194304 | tf_op jit(solution)/shard_map/pack/pallas_call | solution.py:170
  2.6 0.5 collective-permute-start
  3.1 2.5 %collective-permute-start.1 = (bf16[80,384]{1,0:T(8,128)(2,1)S(1)}, bf16[80,384]{1,0:T(8,128)(2,1)S(1)}, u32[]{:S(2)}, u32[]{:S(2)}) collective-permute-start(bf16[80,384]{1,0:T(8,128)(2,1)S(1)} %get-tuple-element.44), channel_id=1, source_target_pairs={{0,4},{1,5},{2,6},{3,7},{4,8},{5,9},{6,10},{7,11},{8,12},{9,13},{1... | collective-permute-start | bytes 184328 | tf_op jit(solution)/shard_map/ppermute | solution.py:679
  5.7 2.4 %collective-permute-start.2 = (bf16[80,384]{1,0:T(8,128)(2,1)S(1)}, bf16[80,384]{1,0:T(8,128)(2,1)S(1)}, u32[]{:S(2)}, u32[]{:S(2)}) collective-permute-start(bf16[80,384]{1,0:T(8,128)(2,1)S(1)} %get-tuple-element.45), channel_id=1, source_target_pairs={{0,5},{1,6},{2,7},{3,4},{4,9},{5,10},{6,11},{7,8},{8,13},{9,14},{1... | collective-permute-start | bytes 184328 | tf_op jit(solution)/shard_map/ppermute | solution.py:679
  8.1 0.0 copy-start.2
  8.1 0.0 copy-start.3
  8.1 2.4 %bias.1.refs_0_.refs_4_ = f32[12,144,144]{2,1,0:T(8,128)S(1)} custom-call(f32[138,2,144]{2,1,0:T(2,128)} %bitcast.16), custom_call_target="tpu_custom_call" | custom-call | flops 1000000000 | bytes 8388608 | tf_op jit(solution)/shard_map/bias/pallas_call | solution.py:266
  10.5 0.0 collective-permute-done.north_ref.refs_1_
  10.5 0.0 copy-done.2
  10.6 0.0 copy-done.3
  10.6 0.0 copy-start
  10.6 0.0 copy-start.1
  10.6 1.8 %near_block.1 = (bf16[288,192]{1,0:T(8,128)(2,1)S(1)}, bf16[288,192]{1,0:T(8,128)(2,1)S(1)}, bf16[288,192]{1,0:T(8,128)(2,1)S(1)}, bf16[12,144,144]{2,1,0:T(8,12...) custom-call(bf16[224,384]{1,0:T(8,128)(2,1)S(1)} %get-tuple-element., ...), custom_call_target="tpu_custom_call" | custom-call | flops 3000000000 | bytes 8388608 | tf_op jit(solution)/shard_map/near_block/pallas_call | solution.py:454
  12.4 0.0 collective-permute-done.1.refs_2_
  12.4 1.0 %collective-permute-done.2.refs_3_ = bf16[80,384]{1,0:T(8,128)(2,1)S(1)} collective-permute-done((bf16[80,384]{1,0:T(8,128)(2,1)S(1)}, bf16[80,384]{1,0:T(8,128)(2,1)S(1)}, u32[]{:S(2)}, u32[]{:S(2)}) %collective-permute-start.2) | collective-permute-done | bytes 61472 | tf_op jit(solution)/shard_map/ppermute | solution.py:679
  13.4 0.0 copy-done
  13.4 0.0 copy-done.1
  13.4 7.6 %block.1 = (bf16[112,384]{1,0:T(8,128)(2,1)S(1)}, bf16[152,384]{1,0:T(8,128)(2,1)S(1)}, bf16[40,384]{1,0:T(8,128)(2,1)S(1)}, f32[1,192]{1,0:T(1,128)S(1)}, f32[2...) custom-call(bf16[224,384]{1,0:T(8,128)(2,1)S(1)} %get-tuple-element.42.own_ref.refs_0_, ...), custom_call_target="tpu_custom_call" | custom-call | flops 8000000000 | bytes 16777216 | tf_op jit(solution)/shard_map/block/pallas_call | solution.py:493
  21.0 0.0 copy-start.4
  21.0 0.2 collective-permute-start.4
  21.2 1.2 %collective-permute-start.3 = (bf16[152,384]{1,0:T(8,128)(2,1)S(1)}, bf16[152,384]{1,0:T(8,128)(2,1)S(1)}, u32[]{:S(2)}, u32[]{:S(2)}) collective-permute-start(bf16[152,384]{1,0:T(8,128)(2,1)S(1)} %get-tuple-element.57), channel_id=1, source_target_pairs={{0,3},{1,0},{2,1},{3,2},{4,7},{5,4},{6,5},{7,6},{8,11},{9,8},{10,9... | collective-permute-start | bytes 350216 | tf_op jit(solution)/shard_map/ppermute | solution.py:679
  22.5 2.4 %collective-permute-done.3.refs_0_.north_ref = bf16[152,384]{1,0:T(8,128)(2,1)S(1)} collective-permute-done((bf16[152,384]{1,0:T(8,128)(2,1)S(1)}, bf16[152,384]{1,0:T(8,128)(2,1)S(1)}, u32[]{:S(2)}, u32[]{:S(2)}) %collective-permute-start.3) | collective-permute-done | bytes 116768 | tf_op jit(solution)/shard_map/ppermute | solution.py:679
  24.8 0.0 collective-permute-done.4.got_ref
  24.9 0.1 core_add.1
  25.0 0.8 %collective-permute-start.5 = (bf16[72,768]{1,0:T(8,128)(2,1)S(1)}, bf16[72,768]{1,0:T(8,128)(2,1)S(1)}, u32[]{:S(2)}, u32[]{:S(2)}) collective-permute-start(bf16[72,768]{1,0:T(8,128)(2,1)S(1)} %get-tuple-element.62), channel_id=1, source_target_pairs={{0,6},{1,7},{2,4},{3,5},{4,2},{5,3},{6,0},{7,1},{8,14},{9,15},{10,... | collective-permute-start | bytes 331784 | tf_op jit(solution)/shard_map/ppermute | solution.py:679
  25.7 0.5 collective-permute-start.6
  26.2 2.3 %collective-permute-start.7 = (bf16[72,768]{1,0:T(8,128)(2,1)S(1)}, bf16[72,768]{1,0:T(8,128)(2,1)S(1)}, u32[]{:S(2)}, u32[]{:S(2)}) collective-permute-start(bf16[72,768]{1,0:T(8,128)(2,1)S(1)} %get-tuple-element.64), channel_id=1, source_target_pairs={{0,4},{1,5},{2,6},{3,7},{4,0},{5,1},{6,2},{7,3},{8,12},{9,13},{10,... | collective-permute-start | bytes 331784 | tf_op jit(solution)/shard_map/ppermute | solution.py:679
  28.5 3.4 %collective-permute-done.5.refs_0_ = bf16[72,768]{1,0:T(8,128)(2,1)S(1)} collective-permute-done((bf16[72,768]{1,0:T(8,128)(2,1)S(1)}, bf16[72,768]{1,0:T(8,128)(2,1)S(1)}, u32[]{:S(2)}, u32[]{:S(2)}) %collective-permute-start.5) | collective-permute-done | bytes 110624 | tf_op jit(solution)/shard_map/ppermute | solution.py:679
  31.9 1.6 %collective-permute-done.6.refs_1_ = bf16[72,768]{1,0:T(8,128)(2,1)S(1)} collective-permute-done((bf16[72,768]{1,0:T(8,128)(2,1)S(1)}, bf16[72,768]{1,0:T(8,128)(2,1)S(1)}, u32[]{:S(2)}, u32[]{:S(2)}) %collective-permute-start.6) | collective-permute-done | bytes 110624 | tf_op jit(solution)/shard_map/ppermute | solution.py:679
  33.5 0.0 collective-permute-done.7.refs_2_
  33.5 0.1 chip_add.1.refs_0_.one_ref
  33.6 0.6 %collective-permute-start.9 = (bf16[440,128]{1,0:T(8,128)(2,1)S(1)}, bf16[440,128]{1,0:T(8,128)(2,1)S(1)}, u32[]{:S(2)}, u32[]{:S(2)}) collective-permute-start(bf16[440,128]{1,0:T(8,128)(2,1)S(1)} %chip_add.1.refs_0_.one_ref), channel_id=1, source_target_pairs={{0,8},{1,9},{2,10},{3,11},{4,12},{5,13},{6,14},{7,15},{8,0},{9,1},... | collective-permute-start | bytes 337928 | tf_op jit(solution)/shard_map/ppermute | solution.py:679
  34.2 3.4 %collective-permute-start.8 = (bf16[80,384]{1,0:T(8,128)(2,1)S(1)}, bf16[80,384]{1,0:T(8,128)(2,1)S(1)}, u32[]{:S(2)}, u32[]{:S(2)}) collective-permute-start(bf16[80,384]{1,0:T(8,128)(2,1)S(1)} %side.1), channel_id=1, source_target_pairs={{0,28},{1,29},{2,30},{3,31},{4,0},{5,1},{6,2},{7,3},{8,4},{9,5},{1... | collective-permute-start | bytes 184328 | tf_op jit(solution)/shard_map/ppermute | solution.py:679
  37.6 1.9 %collective-permute-done.8.side_ref.refs_0_ = bf16[80,384]{1,0:T(8,128)(2,1)S(1)} collective-permute-done((bf16[80,384]{1,0:T(8,128)(2,1)S(1)}, bf16[80,384]{1,0:T(8,128)(2,1)S(1)}, u32[]{:S(2)}, u32[]{:S(2)}) %collective-permute-start.8) | collective-permute-done | bytes 61472 | tf_op jit(solution)/shard_map/ppermute | solution.py:679
  39.5 0.0 collective-permute-done.9.two_ref
  39.5 1.5 %collective-permute-start.10 = (bf16[440,128]{1,0:T(8,128)(2,1)S(1)}, bf16[440,128]{1,0:T(8,128)(2,1)S(1)}, u32[]{:S(2)}, u32[]{:S(2)}) collective-permute-start(bf16[440,128]{1,0:T(8,128)(2,1)S(1)} %deep_add.2.one_ref), channel_id=1, source_target_pairs={{0,16},{1,17},{2,18},{3,19},{4,20},{5,21},{6,22},{7,23},{8,24},{9,... | collective-permute-start | bytes 337928 | tf_op jit(solution)/shard_map/ppermute | solution.py:679
  41.0 0.0 copy-done.4
  41.0 1.2 %to_home.1 = (bf16[576,192]{1,0:T(8,128)(2,1)}, f32[8,128]{1,0:T(8,128)S(1)}) custom-call(bf16[112,384]{1,0:T(8,128)(2,1)S(1)} %get-tuple-element.56.own_ref, bf16[152,384]{1,0:T(8,128)(2,1)S(1)} %collective-permute-done.3.refs_0_.north_ref, bf16[80,384]{1,0:T(8,128)(2,1)S(1)} %collective-permute-done.8.side_ref.refs_0_, s32[1,576]{1,0:T(1,128)S(1)} %copy-done.4), custom_call_target="tpu_custom_call" | custom-call | flops 127401984 | bytes 4194304 | tf_op jit(solution)/shard_map/to_home/pallas_call | solution.py:529
  42.2 4.5 %collective-permute-done.10.two_ref = bf16[440,128]{1,0:T(8,128)(2,1)S(1)} collective-permute-done((bf16[440,128]{1,0:T(8,128)(2,1)S(1)}, bf16[440,128]{1,0:T(8,128)(2,1)S(1)}, u32[]{:S(2)}, u32[]{:S(2)}) %collective-permute-start.10) | collective-permute-done | bytes 112672 | tf_op jit(solution)/shard_map/ppermute | solution.py:679
  46.8 3.0 %collective-permute-start.13 = (bf16[440,128]{1,0:T(8,128)(2,1)S(1)}, bf16[440,128]{1,0:T(8,128)(2,1)S(1)}, u32[]{:S(2)}, u32[]{:S(2)}) collective-permute-start(bf16[440,128]{1,0:T(8,128)(2,1)S(1)} %deep_add.3.refs_0_), channel_id=1, source_target_pairs={{0,6},{1,7},{2,4},{3,5},{4,2},{5,3},{6,0},{7,1},{8,14},{9,15},{10,... | collective-permute-start | bytes 337928 | tf_op jit(solution)/shard_map/ppermute | solution.py:679
  49.8 0.7 %collective-permute-start.12 = (bf16[440,128]{1,0:T(8,128)(2,1)S(1)}, bf16[440,128]{1,0:T(8,128)(2,1)S(1)}, u32[]{:S(2)}, u32[]{:S(2)}) collective-permute-start(bf16[440,128]{1,0:T(8,128)(2,1)S(1)} %deep_add.3.refs_0_), channel_id=1, source_target_pairs={{0,2},{1,3},{2,0},{3,1},{4,6},{5,7},{6,4},{7,5},{8,10},{9,11},{10,... | collective-permute-start | bytes 337928 | tf_op jit(solution)/shard_map/ppermute | solution.py:679
  50.5 0.0 collective-permute-start.11
  50.5 2.3 %collective-permute-done.13.refs_3_ = bf16[440,128]{1,0:T(8,128)(2,1)S(1)} collective-permute-done((bf16[440,128]{1,0:T(8,128)(2,1)S(1)}, bf16[440,128]{1,0:T(8,128)(2,1)S(1)}, u32[]{:S(2)}, u32[]{:S(2)}) %collective-permute-start.13) | collective-permute-done | bytes 112672 | tf_op jit(solution)/shard_map/ppermute | solution.py:679
  52.8 2.1 %collective-permute-done.12.refs_2_ = bf16[440,128]{1,0:T(8,128)(2,1)S(1)} collective-permute-done((bf16[440,128]{1,0:T(8,128)(2,1)S(1)}, bf16[440,128]{1,0:T(8,128)(2,1)S(1)}, u32[]{:S(2)}, u32[]{:S(2)}) %collective-permute-start.12) | collective-permute-done | bytes 112672 | tf_op jit(solution)/shard_map/ppermute | solution.py:679
  54.9 0.3 collective-permute-done.11.refs_1_
  55.3 0.1 join.1.chunks_ref
  55.3 0.1 collective-permute-start.14
  55.4 1.0 %finish_own.1 = (f32[192,576]{1,0:T(8,128)}, f32[192,192]{1,0:T(8,128)}, f32[192,768]{1,0:T(8,128)}, f32[192,768]{1,0:T(8,128)}, f32[1,192]{1,0:T(1,128)S(1)}) custom-call(bf16[1760,128]{1,0:T(8,128)(2,1)S(1)} %join.1.chunks_ref), custom_call_target="tpu_custom_call" | custom-call | flops 1000000 | bytes 2097152 | tf_op jit(solution)/shard_map/finish_own/pallas_call | solution.py:621
  56.5 0.7 %collective-permute-done.14.chunks_ref = bf16[1760,128]{1,0:T(8,128)(2,1)S(1)} collective-permute-done((bf16[1760,128]{1,0:T(8,128)(2,1)S(1)}, bf16[1760,128]{1,0:T(8,128)(2,1)S(1)}, u32[]{:S(2)}, u32[]{:S(2)}) %collective-permute-start.14) | collective-permute-done | bytes 450592 | tf_op jit(solution)/shard_map/ppermute | solution.py:679
  57.2 1.0 %finish_far.1 = (f32[192,576]{1,0:T(8,128)}, f32[192,192]{1,0:T(8,128)}, f32[192,768]{1,0:T(8,128)}, f32[192,768]{1,0:T(8,128)}, f32[1,192]{1,0:T(1,128)}) custom-call(bf16[1760,128]{1,0:T(8,128)(2,1)S(1)} %collective-permute-done.14.chunks_ref, ...), custom_call_target="tpu_custom_call", output_to_operand_aliasing={{0}: (2, {}), {1}: (3, {}), {2}: (4, {}), {3}: (5, {})} | custom-call | flops 1000000 | bytes 2097152 | tf_op jit(solution)/shard_map/finish_far/pallas_call | solution.py:621
  (3 shorter events, 0.1 us)
Async XLA Ops:
  2.6 7.9 %collective-permute-start = (bf16[224,384]{1,0:T(8,128)(2,1)S(1)}, bf16[224,384]{1,0:T(8,128)(2,1)S(1)}, u32[]{:S(2)}, u32[]{:S(2)}) collective-permute-start(bf16[224,384]{1,0:T(8,128)(2,1)S(1)} %get-tuple-element.43), channel_id=1, source_target_pairs={{0,1},{1,2},{2,3},{3,0},{4,5},{5,6},{6,7},{7,4},{8,9},{9,10},{10,1... | collective-permute-start | bytes 516104 | tf_op jit(solution)/shard_map/ppermute | solution.py:679
  3.1 9.2 %collective-permute-start.1 = (bf16[80,384]{1,0:T(8,128)(2,1)S(1)}, bf16[80,384]{1,0:T(8,128)(2,1)S(1)}, u32[]{:S(2)}, u32[]{:S(2)}) collective-permute-start(bf16[80,384]{1,0:T(8,128)(2,1)S(1)} %get-tuple-element.44), channel_id=1, source_target_pairs={{0,4},{1,5},{2,6},{3,7},{4,8},{5,9},{6,10},{7,11},{8,12},{9,13},{1... | collective-permute-start | bytes 184328 | tf_op jit(solution)/shard_map/ppermute | solution.py:679
  5.7 7.7 %collective-permute-start.2 = (bf16[80,384]{1,0:T(8,128)(2,1)S(1)}, bf16[80,384]{1,0:T(8,128)(2,1)S(1)}, u32[]{:S(2)}, u32[]{:S(2)}) collective-permute-start(bf16[80,384]{1,0:T(8,128)(2,1)S(1)} %get-tuple-element.45), channel_id=1, source_target_pairs={{0,5},{1,6},{2,7},{3,4},{4,9},{5,10},{6,11},{7,8},{8,13},{9,14},{1... | collective-permute-start | bytes 184328 | tf_op jit(solution)/shard_map/ppermute | solution.py:679
  8.1 2.4 %copy-start.2 = (bf16[192,576]{1,0:T(8,128)(2,1)S(1)}, bf16[192,576]{1,0:T(8,128)(2,1)}, u32[]{:S(2)}) copy-start(bf16[192,576]{1,0:T(8,128)(2,1)} %refs_5_.1) | copy-start | bytes 663556
  8.1 2.4 %copy-start.3 = (bf16[192,192]{1,0:T(8,128)(2,1)S(1)}, bf16[192,192]{1,0:T(8,128)(2,1)}, u32[]{:S(2)}) copy-start(bf16[192,192]{1,0:T(8,128)(2,1)} %refs_6_.1) | copy-start | bytes 221188
  10.6 2.9 %copy-start = (bf16[192,768]{1,0:T(8,128)(2,1)S(1)}, bf16[192,768]{1,0:T(8,128)(2,1)}, u32[]{:S(2)}) copy-start(bf16[192,768]{1,0:T(8,128)(2,1)} %refs_7_.1) | copy-start | bytes 884740
  10.6 2.9 %copy-start.1 = (bf16[768,192]{0,1:T(8,128)(2,1)S(1)}, bf16[768,192]{0,1:T(8,128)(2,1)}, u32[]{:S(2)}) copy-start(bf16[768,192]{0,1:T(8,128)(2,1)} %param.18) | copy-start | bytes 884740
  21.0 20.0 %copy-start.4 = (s32[1,576]{1,0:T(1,128)S(1)}, s32[1,576]{1,0:T(1,128)}, u32[]{:S(2)}) copy-start(s32[1,576]{1,0:T(1,128)} %constant.5.clone.perm_ref) | copy-start | bytes 6916
  21.0 3.8 %collective-permute-start.4 = (bf16[288,768]{1,0:T(8,128)(2,1)S(1)}, bf16[288,768]{1,0:T(8,128)(2,1)S(1)}, u32[]{:S(2)}, u32[]{:S(2)}) collective-permute-start(bf16[288,768]{1,0:T(8,128)(2,1)S(1)} %get-tuple-element.60), channel_id=1, source_target_pairs={{0,1},{1,0},{2,3},{3,2},{4,5},{5,4},{6,7},{7,6},{8,9},{9,8},{10,11... | collective-permute-start | bytes 1327112 | tf_op jit(solution)/shard_map/ppermute | solution.py:679
  21.2 3.6 %collective-permute-start.3 = (bf16[152,384]{1,0:T(8,128)(2,1)S(1)}, bf16[152,384]{1,0:T(8,128)(2,1)S(1)}, u32[]{:S(2)}, u32[]{:S(2)}) collective-permute-start(bf16[152,384]{1,0:T(8,128)(2,1)S(1)} %get-tuple-element.57), channel_id=1, source_target_pairs={{0,3},{1,0},{2,1},{3,2},{4,7},{5,4},{6,5},{7,6},{8,11},{9,8},{10,9... | collective-permute-start | bytes 350216 | tf_op jit(solution)/shard_map/ppermute | solution.py:679
  25.0 7.0 %collective-permute-start.5 = (bf16[72,768]{1,0:T(8,128)(2,1)S(1)}, bf16[72,768]{1,0:T(8,128)(2,1)S(1)}, u32[]{:S(2)}, u32[]{:S(2)}) collective-permute-start(bf16[72,768]{1,0:T(8,128)(2,1)S(1)} %get-tuple-element.62), channel_id=1, source_target_pairs={{0,6},{1,7},{2,4},{3,5},{4,2},{5,3},{6,0},{7,1},{8,14},{9,15},{10,... | collective-permute-start | bytes 331784 | tf_op jit(solution)/shard_map/ppermute | solution.py:679
  25.7 7.8 %collective-permute-start.6 = (bf16[72,768]{1,0:T(8,128)(2,1)S(1)}, bf16[72,768]{1,0:T(8,128)(2,1)S(1)}, u32[]{:S(2)}, u32[]{:S(2)}) collective-permute-start(bf16[72,768]{1,0:T(8,128)(2,1)S(1)} %get-tuple-element.63), channel_id=1, source_target_pairs={{0,2},{1,3},{2,0},{3,1},{4,6},{5,7},{6,4},{7,5},{8,10},{9,11},{10,... | collective-permute-start | bytes 331784 | tf_op jit(solution)/shard_map/ppermute | solution.py:679
  26.2 7.3 %collective-permute-start.7 = (bf16[72,768]{1,0:T(8,128)(2,1)S(1)}, bf16[72,768]{1,0:T(8,128)(2,1)S(1)}, u32[]{:S(2)}, u32[]{:S(2)}) collective-permute-start(bf16[72,768]{1,0:T(8,128)(2,1)S(1)} %get-tuple-element.64), channel_id=1, source_target_pairs={{0,4},{1,5},{2,6},{3,7},{4,0},{5,1},{6,2},{7,3},{8,12},{9,13},{10,... | collective-permute-start | bytes 331784 | tf_op jit(solution)/shard_map/ppermute | solution.py:679
  33.6 5.9 %collective-permute-start.9 = (bf16[440,128]{1,0:T(8,128)(2,1)S(1)}, bf16[440,128]{1,0:T(8,128)(2,1)S(1)}, u32[]{:S(2)}, u32[]{:S(2)}) collective-permute-start(bf16[440,128]{1,0:T(8,128)(2,1)S(1)} %chip_add.1.refs_0_.one_ref), channel_id=1, source_target_pairs={{0,8},{1,9},{2,10},{3,11},{4,12},{5,13},{6,14},{7,15},{8,0},{9,1},... | collective-permute-start | bytes 337928 | tf_op jit(solution)/shard_map/ppermute | solution.py:679
  34.2 5.3 %collective-permute-start.8 = (bf16[80,384]{1,0:T(8,128)(2,1)S(1)}, bf16[80,384]{1,0:T(8,128)(2,1)S(1)}, u32[]{:S(2)}, u32[]{:S(2)}) collective-permute-start(bf16[80,384]{1,0:T(8,128)(2,1)S(1)} %side.1), channel_id=1, source_target_pairs={{0,28},{1,29},{2,30},{3,31},{4,0},{5,1},{6,2},{7,3},{8,4},{9,5},{1... | collective-permute-start | bytes 184328 | tf_op jit(solution)/shard_map/ppermute | solution.py:679
  39.5 7.2 %collective-permute-start.10 = (bf16[440,128]{1,0:T(8,128)(2,1)S(1)}, bf16[440,128]{1,0:T(8,128)(2,1)S(1)}, u32[]{:S(2)}, u32[]{:S(2)}) collective-permute-start(bf16[440,128]{1,0:T(8,128)(2,1)S(1)} %deep_add.2.one_ref), channel_id=1, source_target_pairs={{0,16},{1,17},{2,18},{3,19},{4,20},{5,21},{6,22},{7,23},{8,24},{9,... | collective-permute-start | bytes 337928 | tf_op jit(solution)/shard_map/ppermute | solution.py:679
  46.8 6.1 %collective-permute-start.13 = (bf16[440,128]{1,0:T(8,128)(2,1)S(1)}, bf16[440,128]{1,0:T(8,128)(2,1)S(1)}, u32[]{:S(2)}, u32[]{:S(2)}) collective-permute-start(bf16[440,128]{1,0:T(8,128)(2,1)S(1)} %deep_add.3.refs_0_), channel_id=1, source_target_pairs={{0,6},{1,7},{2,4},{3,5},{4,2},{5,3},{6,0},{7,1},{8,14},{9,15},{10,... | collective-permute-start | bytes 337928 | tf_op jit(solution)/shard_map/ppermute | solution.py:679
  49.8 5.2 %collective-permute-start.12 = (bf16[440,128]{1,0:T(8,128)(2,1)S(1)}, bf16[440,128]{1,0:T(8,128)(2,1)S(1)}, u32[]{:S(2)}, u32[]{:S(2)}) collective-permute-start(bf16[440,128]{1,0:T(8,128)(2,1)S(1)} %deep_add.3.refs_0_), channel_id=1, source_target_pairs={{0,2},{1,3},{2,0},{3,1},{4,6},{5,7},{6,4},{7,5},{8,10},{9,11},{10,... | collective-permute-start | bytes 337928 | tf_op jit(solution)/shard_map/ppermute | solution.py:679
  50.5 4.8 %collective-permute-start.11 = (bf16[440,128]{1,0:T(8,128)(2,1)S(1)}, bf16[440,128]{1,0:T(8,128)(2,1)S(1)}, u32[]{:S(2)}, u32[]{:S(2)}) collective-permute-start(bf16[440,128]{1,0:T(8,128)(2,1)S(1)} %deep_add.3.refs_0_), channel_id=1, source_target_pairs={{0,4},{1,5},{2,6},{3,7},{4,0},{5,1},{6,2},{7,3},{8,12},{9,13},{10,... | collective-permute-start | bytes 337928 | tf_op jit(solution)/shard_map/ppermute | solution.py:679
  55.3 1.9 %collective-permute-start.14 = (bf16[1760,128]{1,0:T(8,128)(2,1)S(1)}, bf16[1760,128]{1,0:T(8,128)(2,1)S(1)}, u32[]{:S(2)}, u32[]{:S(2)}) collective-permute-start(bf16[1760,128]{1,0:T(8,128)(2,1)S(1)} %join.1.chunks_ref), channel_id=1, source_target_pairs={{0,1},{1,0},{2,3},{3,2},{4,5},{5,4},{6,7},{7,6},{8,9},{9,8},{10,11... | collective-permute-start | bytes 1351688 | tf_op jit(solution)/shard_map/ppermute | solution.py:679

commit v3 on v1

--- a/solution.py
+++ b/solution.py
@@ -132,14 +132,15 @@
 
 
 def pack_kernel(rows, cols, *refs):
-    sources, outs, (tokens_ref, cot_ref, land_ref, vec_ref, perm_ref, sems) = refs[:5], refs[5:-6], refs[-6:]
+    sources, outs, (tokens_ref, cot_ref, land_ref, vec_ref, perm_ref, sems) = refs[:6], refs[6:-7], refs[-6:]
+    targets = (tokens_ref, cot_ref, land_ref, vec_ref, perm_ref, refs[-7])
     copies = [
         pltpu.make_async_copy(source, target, sems.at[n])
-        for n, (source, target) in enumerate(zip(sources, (tokens_ref, cot_ref, land_ref, vec_ref, perm_ref)))
+        for n, (source, target) in enumerate(zip(sources, targets))
     ]
     for copy in copies:
         copy.start()
-    for copy in copies:
+    for copy in copies[:5]:
         copy.wait()
     column = land_column(land_ref, rows, cols)
     added = column * vec_ref[...]
@@ -161,28 +162,34 @@
         row = jnp.broadcast_to(row, (EXTRA, 2 * C))
         out[...] = jnp.concatenate([packed[start : start + count], row], axis=0).astype(bf16)
         start += count
-
-
-def pack(tokens, cotangent, land_sea, vector, rows, cols):
+    copies[5].wait()
+
+
+def pack(tokens, cotangent, land_sea, vector, table, rows, cols):
+    flat = table[0].transpose(1, 3, 0, 2).reshape(HEADS * RELW, table.shape[1], PLACES * PLACES)
     parts = piece_rows(rows, cols)
     perm = spots(np.concatenate(parts))
     count = Z * rows * cols
     return pl.pallas_call(
         functools.partial(pack_kernel, rows, cols),
-        out_shape=[shape((part.size + EXTRA, 2 * C), bf16) for part in parts],
-        in_specs=[pl.BlockSpec(memory_space=pltpu.HBM)] * 5,
-        out_specs=vmem(4),
+        out_shape=[shape((part.size + EXTRA, 2 * C), bf16) for part in parts] + [shape(flat.shape, f32)],
+        in_specs=[pl.BlockSpec(memory_space=pltpu.HBM)] * 6,
+        out_specs=vmem(5),
         scratch_shapes=[
             pltpu.VMEM((count, C), bf16),
             pltpu.VMEM((count, C), bf16),
             pltpu.VMEM((rows, cols), jnp.int32),
             pltpu.VMEM((1, C), f32),
             pltpu.VMEM((1, count), jnp.int32),
-            pltpu.SemaphoreType.DMA((5,)),
+            pltpu.SemaphoreType.DMA((6,)),
         ],
+        compiler_params=pltpu.CompilerParams(vmem_limit_bytes=24 * MIB),
         cost_estimate=cost(4 * count * count * C, 4 * MIB),
         name="pack",
-    )(tokens.reshape(count, C), cotangent.reshape(count, C), land_sea, vector.reshape(1, C), perm)
+    )(*[
+        pltpu.with_memory_space_constraint(value, pltpu.HBM)
+        for value in (tokens.reshape(count, C), cotangent.reshape(count, C), land_sea, vector.reshape(1, C), perm, flat)
+    ])
 
 
 def floor_div(values, divisor):
@@ -251,11 +258,10 @@
                 out_ref[g, half * RUN + w * SPOTS : half * RUN + (w + 1) * SPOTS, :] = rows
 
 
-def expand_bias(table):
-    levels = table.shape[1]
+def expand_bias(flat):
+    levels = flat.shape[1]
     groups = levels * HEADS
     pairs = PLACES * PLACES
-    flat = table[0].transpose(1, 3, 0, 2).reshape(HEADS * RELW, levels, pairs)
     return pl.pallas_call(
         functools.partial(bias_kernel, levels),
         out_shape=shape((groups, TOK, TOK), f32),
@@ -679,11 +685,11 @@
     shift = functools.partial(send, lon_count=lon_count, lat_count=lat_count)
     lon_windows = cols // WW
 
-    own, north, side, corner = pack(tokens, cotangent, land_sea, land_vector, rows, cols)
+    own, north, side, corner, table = pack(tokens, cotangent, land_sea, land_vector, earth_bias, rows, cols)
     north = shift(north, move=lambda lon, lat: (lon, lat + 1))
     side = shift(side, move=lambda lon, lat: (lon + 1, lat))
     corner = shift(corner, move=lambda lon, lat: (lon + 1, lat + 1))
-    bias = expand_bias(earth_bias)
+    bias = expand_bias(table)
 
     sizes = [part.size for part in piece_rows(rows, cols)]
     pieces = (own, north, side, corner)

time: 59.2 us -> 58.3 us (0.985)
  local copies, waits for them, and re-layouts: 0.99 us -> 0.03 us
  waiting for transfers between devices: 20.5 us -> 21.4 us
  Pallas kernels: 17 us -> 16.4 us
    unnamed x14 -> x10, local copies, waits for them, and re-layouts: 0.99 us -> 0.03 us
    ppermute x15, waiting for transfers between devices: 20.5 us -> 21.4 us  [send(): return lax.ppermute(value, AXES, pairs)]
    pallas_call x1, Pallas kernels: 2.67 us -> 2.01 us  [pack(): pl.pallas_call(functools.partial(pack_kernel, rows, cols), out_shape=[sha...]
where the time goes in v3:
time: 58.3 us; the launch traced here: 58.2 us
  waiting for transfers between devices  21.4 us (37%)
  starting transfers between devices  19.6 us (34%)
  Pallas kernels  16.4 us (28%)
  between operations  0.78 us (1%)
    ppermute x15, waiting for transfers between devices, send(): return lax.ppermute(value, AXES, pairs)  21.4 us
    ppermute x15, starting transfers between devices, send(): return lax.ppermute(value, AXES, pairs)  19.6 us
    pallas_call x1, Pallas kernels, block(): pl.pallas_call(functools.partial(block_kernel, lon_windows, sizes), out_s...  7.57 us
    pallas_call x2, Pallas kernels, finish(): pl.pallas_call(functools.partial(finish_kernel, bool(before)), out_shape=...  2.08 us
    pallas_call x1, Pallas kernels, pack(): pl.pallas_call(functools.partial(pack_kernel, rows, cols), out_shape=[sha...  2.01 us
    pallas_call x1, Pallas kernels, near_block(): pl.pallas_call(functools.partial(near_kernel, lon_windows), out_shape=[sh...  1.78 us
    pallas_call x1, Pallas kernels, expand_bias(): pl.pallas_call(functools.partial(bias_kernel, levels), out_shape=shape((g...  1.42 us
    pallas_call x1, Pallas kernels, to_home(): pl.pallas_call(functools.partial(home_kernel, sizes), out_shape=[shape((c...  1.19 us
  transfers between devices with their start and end apart: 15, of which 11 were waited for; matrix products, arithmetic and copies ran while one was open for 0% of the time, Pallas kernels for 9%

profile of v3, /device:TPU:0, one launch (start us, length us, event | category | flops | bytes accessed | tf_op | source)
XLA Modules:
  0.0 58.2 jit_solution(12877174531702772754)
XLA Ops:
  0.6 2.0 %pack.1 = (bf16[224,384]{1,0:T(8,128)(2,1)S(1)}, bf16[224,384]{1,0:T(8,128)(2,1)S(1)}, bf16[80,384]{1,0:T(8,128)(2,1)S(1)}, bf16[80,384]{1,0:T(8,128)(2,1)S(1)}, f32[138,2,144]{2,1,0:T(2,128)S(1)}) custom-call(bf16[576,192]{1,0:T(8,128)(2,1)} %bitcast.14, bf16[576,192]{1,0:T(8,128)(2,1)} %bitcast.15, s32[6,24]{1,0:T(8,128)} %refs_2_.2, f32[1,192]{1,0:T(1,128)} %bitcast.17, ...), custom_call_target="tpu_custom_call" | custom-call | flops 254803968 | bytes 4194304 | tf_op jit(solution)/shard_map/pack/pallas_call | solution.py:173
  2.6 0.5 collective-permute-start
  3.2 2.6 %collective-permute-start.1 = (bf16[80,384]{1,0:T(8,128)(2,1)S(1)}, bf16[80,384]{1,0:T(8,128)(2,1)S(1)}, u32[]{:S(2)}, u32[]{:S(2)}) collective-permute-start(bf16[80,384]{1,0:T(8,128)(2,1)S(1)} %get-tuple-element.45), channel_id=1, source_target_pairs={{0,4},{1,5},{2,6},{3,7},{4,8},{5,9},{6,10},{7,11},{8,12},{9,13},{1... | collective-permute-start | bytes 184328 | tf_op jit(solution)/shard_map/ppermute | solution.py:677
  5.7 2.4 %collective-permute-start.2 = (bf16[80,384]{1,0:T(8,128)(2,1)S(1)}, bf16[80,384]{1,0:T(8,128)(2,1)S(1)}, u32[]{:S(2)}, u32[]{:S(2)}) collective-permute-start(bf16[80,384]{1,0:T(8,128)(2,1)S(1)} %get-tuple-element.46), channel_id=1, source_target_pairs={{0,5},{1,6},{2,7},{3,4},{4,9},{5,10},{6,11},{7,8},{8,13},{9,14},{1... | collective-permute-start | bytes 184328 | tf_op jit(solution)/shard_map/ppermute | solution.py:677
  8.1 0.0 copy-start.2
  8.2 0.0 copy-start.3
  8.2 1.4 %bias.1.refs_0_.refs_4_ = f32[12,144,144]{2,1,0:T(8,128)S(1)} custom-call(f32[138,2,144]{2,1,0:T(2,128)S(1)} %get-tuple-element.47.table_ref), custom_call_target="tpu_custom_call" | custom-call | flops 1000000000 | bytes 8388608 | tf_op jit(solution)/shard_map/bias/pallas_call | solution.py:265
  9.6 0.0 collective-permute-done.north_ref.refs_1_
  9.6 0.0 copy-done.2
  9.6 0.0 copy-done.3
  9.6 0.0 copy-start
  9.6 0.0 copy-start.1
  9.6 1.8 %near_block.1 = (bf16[288,192]{1,0:T(8,128)(2,1)S(1)}, bf16[288,192]{1,0:T(8,128)(2,1)S(1)}, bf16[288,192]{1,0:T(8,128)(2,1)S(1)}, bf16[12,144,144]{2,1,0:T(8,12...) custom-call(bf16[224,384]{1,0:T(8,128)(2,1)S(1)} %get-tuple-element., ...), custom_call_target="tpu_custom_call" | custom-call | flops 3000000000 | bytes 8388608 | tf_op jit(solution)/shard_map/near_block/pallas_call | solution.py:452
  11.4 0.0 collective-permute-done.1.refs_2_
  11.4 2.0 %collective-permute-done.2.refs_3_ = bf16[80,384]{1,0:T(8,128)(2,1)S(1)} collective-permute-done((bf16[80,384]{1,0:T(8,128)(2,1)S(1)}, bf16[80,384]{1,0:T(8,128)(2,1)S(1)}, u32[]{:S(2)}, u32[]{:S(2)}) %collective-permute-start.2) | collective-permute-done | bytes 61472 | tf_op jit(solution)/shard_map/ppermute | solution.py:677
  13.4 0.0 copy-done
  13.4 0.0 copy-done.1
  13.4 7.6 %block.1 = (bf16[112,384]{1,0:T(8,128)(2,1)S(1)}, bf16[152,384]{1,0:T(8,128)(2,1)S(1)}, bf16[40,384]{1,0:T(8,128)(2,1)S(1)}, f32[1,192]{1,0:T(1,128)S(1)}, f32[2...) custom-call(bf16[224,384]{1,0:T(8,128)(2,1)S(1)} %get-tuple-element.43.own_ref.refs_0_, ...), custom_call_target="tpu_custom_call" | custom-call | flops 8000000000 | bytes 16777216 | tf_op jit(solution)/shard_map/block/pallas_call | solution.py:491
  21.0 0.0 copy-start.4
  21.0 0.2 collective-permute-start.4
  21.2 1.3 %collective-permute-start.3 = (bf16[152,384]{1,0:T(8,128)(2,1)S(1)}, bf16[152,384]{1,0:T(8,128)(2,1)S(1)}, u32[]{:S(2)}, u32[]{:S(2)}) collective-permute-start(bf16[152,384]{1,0:T(8,128)(2,1)S(1)} %get-tuple-element.59), channel_id=1, source_target_pairs={{0,3},{1,0},{2,1},{3,2},{4,7},{5,4},{6,5},{7,6},{8,11},{9,8},{10,9... | collective-permute-start | bytes 350216 | tf_op jit(solution)/shard_map/ppermute | solution.py:677
  22.5 2.4 %collective-permute-done.3.refs_0_.north_ref = bf16[152,384]{1,0:T(8,128)(2,1)S(1)} collective-permute-done((bf16[152,384]{1,0:T(8,128)(2,1)S(1)}, bf16[152,384]{1,0:T(8,128)(2,1)S(1)}, u32[]{:S(2)}, u32[]{:S(2)}) %collective-permute-start.3) | collective-permute-done | bytes 116768 | tf_op jit(solution)/shard_map/ppermute | solution.py:677
  24.9 0.0 collective-permute-done.4.got_ref
  24.9 0.1 core_add.1
  25.0 0.1 collective-permute-start.5
  25.0 0.8 %collective-permute-start.6 = (bf16[72,768]{1,0:T(8,128)(2,1)S(1)}, bf16[72,768]{1,0:T(8,128)(2,1)S(1)}, u32[]{:S(2)}, u32[]{:S(2)}) collective-permute-start(bf16[72,768]{1,0:T(8,128)(2,1)S(1)} %get-tuple-element.65), channel_id=1, source_target_pairs={{0,2},{1,3},{2,0},{3,1},{4,6},{5,7},{6,4},{7,5},{8,10},{9,11},{10,... | collective-permute-start | bytes 331784 | tf_op jit(solution)/shard_map/ppermute | solution.py:677
  25.9 2.6 %collective-permute-start.7 = (bf16[72,768]{1,0:T(8,128)(2,1)S(1)}, bf16[72,768]{1,0:T(8,128)(2,1)S(1)}, u32[]{:S(2)}, u32[]{:S(2)}) collective-permute-start(bf16[72,768]{1,0:T(8,128)(2,1)S(1)} %get-tuple-element.66), channel_id=1, source_target_pairs={{0,4},{1,5},{2,6},{3,7},{4,0},{5,1},{6,2},{7,3},{8,12},{9,13},{10,... | collective-permute-start | bytes 331784 | tf_op jit(solution)/shard_map/ppermute | solution.py:677
  28.5 3.4 %collective-permute-done.5.refs_0_ = bf16[72,768]{1,0:T(8,128)(2,1)S(1)} collective-permute-done((bf16[72,768]{1,0:T(8,128)(2,1)S(1)}, bf16[72,768]{1,0:T(8,128)(2,1)S(1)}, u32[]{:S(2)}, u32[]{:S(2)}) %collective-permute-start.5) | collective-permute-done | bytes 110624 | tf_op jit(solution)/shard_map/ppermute | solution.py:677
  31.9 1.4 %collective-permute-done.6.refs_1_ = bf16[72,768]{1,0:T(8,128)(2,1)S(1)} collective-permute-done((bf16[72,768]{1,0:T(8,128)(2,1)S(1)}, bf16[72,768]{1,0:T(8,128)(2,1)S(1)}, u32[]{:S(2)}, u32[]{:S(2)}) %collective-permute-start.6) | collective-permute-done | bytes 110624 | tf_op jit(solution)/shard_map/ppermute | solution.py:677
  33.4 0.0 collective-permute-done.7.refs_2_
  33.4 0.1 chip_add.1.refs_0_.one_ref
  33.5 0.6 collective-permute-start.9
  34.0 3.0 %collective-permute-start.8 = (bf16[80,384]{1,0:T(8,128)(2,1)S(1)}, bf16[80,384]{1,0:T(8,128)(2,1)S(1)}, u32[]{:S(2)}, u32[]{:S(2)}) collective-permute-start(bf16[80,384]{1,0:T(8,128)(2,1)S(1)} %side.1), channel_id=1, source_target_pairs={{0,28},{1,29},{2,30},{3,31},{4,0},{5,1},{6,2},{7,3},{8,4},{9,5},{1... | collective-permute-start | bytes 184328 | tf_op jit(solution)/shard_map/ppermute | solution.py:677
  37.0 1.9 %collective-permute-done.8.side_ref.refs_0_ = bf16[80,384]{1,0:T(8,128)(2,1)S(1)} collective-permute-done((bf16[80,384]{1,0:T(8,128)(2,1)S(1)}, bf16[80,384]{1,0:T(8,128)(2,1)S(1)}, u32[]{:S(2)}, u32[]{:S(2)}) %collective-permute-start.8) | collective-permute-done | bytes 61472 | tf_op jit(solution)/shard_map/ppermute | solution.py:677
  38.9 0.4 collective-permute-done.9.two_ref
  39.3 1.6 %collective-permute-start.10 = (bf16[440,128]{1,0:T(8,128)(2,1)S(1)}, bf16[440,128]{1,0:T(8,128)(2,1)S(1)}, u32[]{:S(2)}, u32[]{:S(2)}) collective-permute-start(bf16[440,128]{1,0:T(8,128)(2,1)S(1)} %deep_add.2.one_ref), channel_id=1, source_target_pairs={{0,16},{1,17},{2,18},{3,19},{4,20},{5,21},{6,22},{7,23},{8,24},{9,... | collective-permute-start | bytes 337928 | tf_op jit(solution)/shard_map/ppermute | solution.py:677
  40.9 0.0 copy-done.4
  40.9 1.2 %to_home.1 = (bf16[576,192]{1,0:T(8,128)(2,1)}, f32[8,128]{1,0:T(8,128)S(1)}) custom-call(bf16[112,384]{1,0:T(8,128)(2,1)S(1)} %get-tuple-element.58.own_ref, bf16[152,384]{1,0:T(8,128)(2,1)S(1)} %collective-permute-done.3.refs_0_.north_ref, bf16[80,384]{1,0:T(8,128)(2,1)S(1)} %collective-permute-done.8.side_ref.refs_0_, s32[1,576]{1,0:T(1,128)S(1)} %copy-done.4), custom_call_target="tpu_custom_call" | custom-call | flops 127401984 | bytes 4194304 | tf_op jit(solution)/shard_map/to_home/pallas_call | solution.py:527
  42.1 4.3 %collective-permute-done.10.two_ref = bf16[440,128]{1,0:T(8,128)(2,1)S(1)} collective-permute-done((bf16[440,128]{1,0:T(8,128)(2,1)S(1)}, bf16[440,128]{1,0:T(8,128)(2,1)S(1)}, u32[]{:S(2)}, u32[]{:S(2)}) %collective-permute-start.10) | collective-permute-done | bytes 112672 | tf_op jit(solution)/shard_map/ppermute | solution.py:677
  46.4 3.2 %collective-permute-start.13 = (bf16[440,128]{1,0:T(8,128)(2,1)S(1)}, bf16[440,128]{1,0:T(8,128)(2,1)S(1)}, u32[]{:S(2)}, u32[]{:S(2)}) collective-permute-start(bf16[440,128]{1,0:T(8,128)(2,1)S(1)} %deep_add.3.refs_0_), channel_id=1, source_target_pairs={{0,6},{1,7},{2,4},{3,5},{4,2},{5,3},{6,0},{7,1},{8,14},{9,15},{10,... | collective-permute-start | bytes 337928 | tf_op jit(solution)/shard_map/ppermute | solution.py:677
  49.6 0.8 %collective-permute-start.12 = (bf16[440,128]{1,0:T(8,128)(2,1)S(1)}, bf16[440,128]{1,0:T(8,128)(2,1)S(1)}, u32[]{:S(2)}, u32[]{:S(2)}) collective-permute-start(bf16[440,128]{1,0:T(8,128)(2,1)S(1)} %deep_add.3.refs_0_), channel_id=1, source_target_pairs={{0,2},{1,3},{2,0},{3,1},{4,6},{5,7},{6,4},{7,5},{8,10},{9,11},{10,... | collective-permute-start | bytes 337928 | tf_op jit(solution)/shard_map/ppermute | solution.py:677
  50.4 0.0 collective-permute-start.11
  50.4 2.2 %collective-permute-done.13.refs_3_ = bf16[440,128]{1,0:T(8,128)(2,1)S(1)} collective-permute-done((bf16[440,128]{1,0:T(8,128)(2,1)S(1)}, bf16[440,128]{1,0:T(8,128)(2,1)S(1)}, u32[]{:S(2)}, u32[]{:S(2)}) %collective-permute-start.13) | collective-permute-done | bytes 112672 | tf_op jit(solution)/shard_map/ppermute | solution.py:677
  52.6 2.1 %collective-permute-done.12.refs_2_ = bf16[440,128]{1,0:T(8,128)(2,1)S(1)} collective-permute-done((bf16[440,128]{1,0:T(8,128)(2,1)S(1)}, bf16[440,128]{1,0:T(8,128)(2,1)S(1)}, u32[]{:S(2)}, u32[]{:S(2)}) %collective-permute-start.12) | collective-permute-done | bytes 112672 | tf_op jit(solution)/shard_map/ppermute | solution.py:677
  54.7 0.5 collective-permute-done.11.refs_1_
  55.2 0.1 join.1.chunks_ref
  55.2 0.1 collective-permute-start.14
  55.3 1.0 %finish_own.1 = (f32[192,576]{1,0:T(8,128)}, f32[192,192]{1,0:T(8,128)}, f32[192,768]{1,0:T(8,128)}, f32[192,768]{1,0:T(8,128)}, f32[1,192]{1,0:T(1,128)S(1)}) custom-call(bf16[1760,128]{1,0:T(8,128)(2,1)S(1)} %join.1.chunks_ref), custom_call_target="tpu_custom_call" | custom-call | flops 1000000 | bytes 2097152 | tf_op jit(solution)/shard_map/finish_own/pallas_call | solution.py:619
  56.4 0.7 %collective-permute-done.14.chunks_ref = bf16[1760,128]{1,0:T(8,128)(2,1)S(1)} collective-permute-done((bf16[1760,128]{1,0:T(8,128)(2,1)S(1)}, bf16[1760,128]{1,0:T(8,128)(2,1)S(1)}, u32[]{:S(2)}, u32[]{:S(2)}) %collective-permute-start.14) | collective-permute-done | bytes 450592 | tf_op jit(solution)/shard_map/ppermute | solution.py:677
  57.1 1.0 %finish_far.1 = (f32[192,576]{1,0:T(8,128)}, f32[192,192]{1,0:T(8,128)}, f32[192,768]{1,0:T(8,128)}, f32[192,768]{1,0:T(8,128)}, f32[1,192]{1,0:T(1,128)}) custom-call(bf16[1760,128]{1,0:T(8,128)(2,1)S(1)} %collective-permute-done.14.chunks_ref, ...), custom_call_target="tpu_custom_call", output_to_operand_aliasing={{0}: (2, {}), {1}: (3, {}), {2}: (4, {}), {3}: (5, {})} | custom-call | flops 1000000 | bytes 2097152 | tf_op jit(solution)/shard_map/finish_far/pallas_call | solution.py:619
  (3 shorter events, 0.1 us)
Async XLA Ops:
  2.6 6.9 %collective-permute-start = (bf16[224,384]{1,0:T(8,128)(2,1)S(1)}, bf16[224,384]{1,0:T(8,128)(2,1)S(1)}, u32[]{:S(2)}, u32[]{:S(2)}) collective-permute-start(bf16[224,384]{1,0:T(8,128)(2,1)S(1)} %get-tuple-element.44), channel_id=1, source_target_pairs={{0,1},{1,2},{2,3},{3,0},{4,5},{5,6},{6,7},{7,4},{8,9},{9,10},{10,1... | collective-permute-start | bytes 516104 | tf_op jit(solution)/shard_map/ppermute | solution.py:677
  3.2 8.3 %collective-permute-start.1 = (bf16[80,384]{1,0:T(8,128)(2,1)S(1)}, bf16[80,384]{1,0:T(8,128)(2,1)S(1)}, u32[]{:S(2)}, u32[]{:S(2)}) collective-permute-start(bf16[80,384]{1,0:T(8,128)(2,1)S(1)} %get-tuple-element.45), channel_id=1, source_target_pairs={{0,4},{1,5},{2,6},{3,7},{4,8},{5,9},{6,10},{7,11},{8,12},{9,13},{1... | collective-permute-start | bytes 184328 | tf_op jit(solution)/shard_map/ppermute | solution.py:677
  5.7 7.7 %collective-permute-start.2 = (bf16[80,384]{1,0:T(8,128)(2,1)S(1)}, bf16[80,384]{1,0:T(8,128)(2,1)S(1)}, u32[]{:S(2)}, u32[]{:S(2)}) collective-permute-start(bf16[80,384]{1,0:T(8,128)(2,1)S(1)} %get-tuple-element.46), channel_id=1, source_target_pairs={{0,5},{1,6},{2,7},{3,4},{4,9},{5,10},{6,11},{7,8},{8,13},{9,14},{1... | collective-permute-start | bytes 184328 | tf_op jit(solution)/shard_map/ppermute | solution.py:677
  8.1 1.4 %copy-start.2 = (bf16[192,576]{1,0:T(8,128)(2,1)S(1)}, bf16[192,576]{1,0:T(8,128)(2,1)}, u32[]{:S(2)}) copy-start(bf16[192,576]{1,0:T(8,128)(2,1)} %refs_5_.1) | copy-start | bytes 663556
  8.2 1.5 %copy-start.3 = (bf16[192,192]{1,0:T(8,128)(2,1)S(1)}, bf16[192,192]{1,0:T(8,128)(2,1)}, u32[]{:S(2)}) copy-start(bf16[192,192]{1,0:T(8,128)(2,1)} %refs_6_.1) | copy-start | bytes 221188
  9.6 3.8 %copy-start = (bf16[192,768]{1,0:T(8,128)(2,1)S(1)}, bf16[192,768]{1,0:T(8,128)(2,1)}, u32[]{:S(2)}) copy-start(bf16[192,768]{1,0:T(8,128)(2,1)} %refs_7_.1) | copy-start | bytes 884740
  9.6 3.8 %copy-start.1 = (bf16[768,192]{0,1:T(8,128)(2,1)S(1)}, bf16[768,192]{0,1:T(8,128)(2,1)}, u32[]{:S(2)}) copy-start(bf16[768,192]{0,1:T(8,128)(2,1)} %param.18) | copy-start | bytes 884740
  21.0 19.9 %copy-start.4 = (s32[1,576]{1,0:T(1,128)S(1)}, s32[1,576]{1,0:T(1,128)}, u32[]{:S(2)}) copy-start(s32[1,576]{1,0:T(1,128)} %constant.5.clone.perm_ref) | copy-start | bytes 6916
  21.0 3.8 %collective-permute-start.4 = (bf16[288,768]{1,0:T(8,128)(2,1)S(1)}, bf16[288,768]{1,0:T(8,128)(2,1)S(1)}, u32[]{:S(2)}, u32[]{:S(2)}) collective-permute-start(bf16[288,768]{1,0:T(8,128)(2,1)S(1)} %get-tuple-element.62), channel_id=1, source_target_pairs={{0,1},{1,0},{2,3},{3,2},{4,5},{5,4},{6,7},{7,6},{8,9},{9,8},{10,11... | collective-permute-start | bytes 1327112 | tf_op jit(solution)/shard_map/ppermute | solution.py:677
  21.2 3.6 %collective-permute-start.3 = (bf16[152,384]{1,0:T(8,128)(2,1)S(1)}, bf16[152,384]{1,0:T(8,128)(2,1)S(1)}, u32[]{:S(2)}, u32[]{:S(2)}) collective-permute-start(bf16[152,384]{1,0:T(8,128)(2,1)S(1)} %get-tuple-element.59), channel_id=1, source_target_pairs={{0,3},{1,0},{2,1},{3,2},{4,7},{5,4},{6,5},{7,6},{8,11},{9,8},{10,9... | collective-permute-start | bytes 350216 | tf_op jit(solution)/shard_map/ppermute | solution.py:677
  25.0 7.0 %collective-permute-start.5 = (bf16[72,768]{1,0:T(8,128)(2,1)S(1)}, bf16[72,768]{1,0:T(8,128)(2,1)S(1)}, u32[]{:S(2)}, u32[]{:S(2)}) collective-permute-start(bf16[72,768]{1,0:T(8,128)(2,1)S(1)} %get-tuple-element.64), channel_id=1, source_target_pairs={{0,6},{1,7},{2,4},{3,5},{4,2},{5,3},{6,0},{7,1},{8,14},{9,15},{10,... | collective-permute-start | bytes 331784 | tf_op jit(solution)/shard_map/ppermute | solution.py:677
  25.0 8.3 %collective-permute-start.6 = (bf16[72,768]{1,0:T(8,128)(2,1)S(1)}, bf16[72,768]{1,0:T(8,128)(2,1)S(1)}, u32[]{:S(2)}, u32[]{:S(2)}) collective-permute-start(bf16[72,768]{1,0:T(8,128)(2,1)S(1)} %get-tuple-element.65), channel_id=1, source_target_pairs={{0,2},{1,3},{2,0},{3,1},{4,6},{5,7},{6,4},{7,5},{8,10},{9,11},{10,... | collective-permute-start | bytes 331784 | tf_op jit(solution)/shard_map/ppermute | solution.py:677
  25.9 7.5 %collective-permute-start.7 = (bf16[72,768]{1,0:T(8,128)(2,1)S(1)}, bf16[72,768]{1,0:T(8,128)(2,1)S(1)}, u32[]{:S(2)}, u32[]{:S(2)}) collective-permute-start(bf16[72,768]{1,0:T(8,128)(2,1)S(1)} %get-tuple-element.66), channel_id=1, source_target_pairs={{0,4},{1,5},{2,6},{3,7},{4,0},{5,1},{6,2},{7,3},{8,12},{9,13},{10,... | collective-permute-start | bytes 331784 | tf_op jit(solution)/shard_map/ppermute | solution.py:677
  33.5 5.8 %collective-permute-start.9 = (bf16[440,128]{1,0:T(8,128)(2,1)S(1)}, bf16[440,128]{1,0:T(8,128)(2,1)S(1)}, u32[]{:S(2)}, u32[]{:S(2)}) collective-permute-start(bf16[440,128]{1,0:T(8,128)(2,1)S(1)} %chip_add.1.refs_0_.one_ref), channel_id=1, source_target_pairs={{0,8},{1,9},{2,10},{3,11},{4,12},{5,13},{6,14},{7,15},{8,0},{9,1},... | collective-permute-start | bytes 337928 | tf_op jit(solution)/shard_map/ppermute | solution.py:677
  34.0 4.8 %collective-permute-start.8 = (bf16[80,384]{1,0:T(8,128)(2,1)S(1)}, bf16[80,384]{1,0:T(8,128)(2,1)S(1)}, u32[]{:S(2)}, u32[]{:S(2)}) collective-permute-start(bf16[80,384]{1,0:T(8,128)(2,1)S(1)} %side.1), channel_id=1, source_target_pairs={{0,28},{1,29},{2,30},{3,31},{4,0},{5,1},{6,2},{7,3},{8,4},{9,5},{1... | collective-permute-start | bytes 184328 | tf_op jit(solution)/shard_map/ppermute | solution.py:677
  39.3 7.0 %collective-permute-start.10 = (bf16[440,128]{1,0:T(8,128)(2,1)S(1)}, bf16[440,128]{1,0:T(8,128)(2,1)S(1)}, u32[]{:S(2)}, u32[]{:S(2)}) collective-permute-start(bf16[440,128]{1,0:T(8,128)(2,1)S(1)} %deep_add.2.one_ref), channel_id=1, source_target_pairs={{0,16},{1,17},{2,18},{3,19},{4,20},{5,21},{6,22},{7,23},{8,24},{9,... | collective-permute-start | bytes 337928 | tf_op jit(solution)/shard_map/ppermute | solution.py:677
  46.4 6.2 %collective-permute-start.13 = (bf16[440,128]{1,0:T(8,128)(2,1)S(1)}, bf16[440,128]{1,0:T(8,128)(2,1)S(1)}, u32[]{:S(2)}, u32[]{:S(2)}) collective-permute-start(bf16[440,128]{1,0:T(8,128)(2,1)S(1)} %deep_add.3.refs_0_), channel_id=1, source_target_pairs={{0,6},{1,7},{2,4},{3,5},{4,2},{5,3},{6,0},{7,1},{8,14},{9,15},{10,... | collective-permute-start | bytes 337928 | tf_op jit(solution)/shard_map/ppermute | solution.py:677
  49.6 5.0 %collective-permute-start.12 = (bf16[440,128]{1,0:T(8,128)(2,1)S(1)}, bf16[440,128]{1,0:T(8,128)(2,1)S(1)}, u32[]{:S(2)}, u32[]{:S(2)}) collective-permute-start(bf16[440,128]{1,0:T(8,128)(2,1)S(1)} %deep_add.3.refs_0_), channel_id=1, source_target_pairs={{0,2},{1,3},{2,0},{3,1},{4,6},{5,7},{6,4},{7,5},{8,10},{9,11},{10,... | collective-permute-start | bytes 337928 | tf_op jit(solution)/shard_map/ppermute | solution.py:677
  50.4 4.8 %collective-permute-start.11 = (bf16[440,128]{1,0:T(8,128)(2,1)S(1)}, bf16[440,128]{1,0:T(8,128)(2,1)S(1)}, u32[]{:S(2)}, u32[]{:S(2)}) collective-permute-start(bf16[440,128]{1,0:T(8,128)(2,1)S(1)} %deep_add.3.refs_0_), channel_id=1, source_target_pairs={{0,4},{1,5},{2,6},{3,7},{4,0},{5,1},{6,2},{7,3},{8,12},{9,13},{10,... | collective-permute-start | bytes 337928 | tf_op jit(solution)/shard_map/ppermute | solution.py:677
  55.2 1.9 %collective-permute-start.14 = (bf16[1760,128]{1,0:T(8,128)(2,1)S(1)}, bf16[1760,128]{1,0:T(8,128)(2,1)S(1)}, u32[]{:S(2)}, u32[]{:S(2)}) collective-permute-start(bf16[1760,128]{1,0:T(8,128)(2,1)S(1)} %join.1.chunks_ref), channel_id=1, source_target_pairs={{0,1},{1,0},{2,3},{3,2},{4,5},{5,4},{6,7},{7,6},{8,9},{9,8},{10,11... | collective-permute-start | bytes 1351688 | tf_op jit(solution)/shard_map/ppermute | solution.py:677
